TPU v7x, 512 devices: a whole 4x8x8 slice. The times are simulated.
512 devices in a mesh: enc: 64 (over y, x, core), mdl: 8 (over z).
Axes of the slice: x: 4, y: 8, z: 8, core: 2. Of those that a mesh axis runs over, the one named last changes fastest.
Arguments:
- tile_feats: bfloat16 [256, 8, 8, 1536], P('enc'), may hold values from -6 to 6
- dw_weight: bfloat16 [7, 7, 1536], replicated, may hold values from -0.875 to 0.875
- ln_gain: float32 [1536], replicated, may hold values from 0.25 to 1.75
- w_expand: bfloat16 [1536, 6144], P('enc', 'mdl'), may hold values from -0.15625 to 0.15625
- w_contract: bfloat16 [1536, 6144], P('enc', 'mdl'), may hold values from -0.078125 to 0.078125
- layer_scale: float32 [1536], replicated, may hold values from 0.3 to 2
- tile_owner: int32 [256, 1], P('enc'), may hold values from 0 to 63
- tissue_index: int32 [64, 256], P('enc'), may hold values from 0 to 255, each once within a row
- slide_embed: bfloat16 [16384, 1536], P('enc'), may hold values from -6 to 6
- slide_gain: float32 [1536], replicated, may hold values from 0.25 to 1.75
- w_query: bfloat16 [1536, 768], P(None, 'mdl')
- w_key: bfloat16 [1536, 768], P(None, 'mdl')
- w_value: bfloat16 [1536, 768], P(None, 'mdl'), may hold values from -0.15625 to 0.15625
- w_out: bfloat16 [768, 1536], P('mdl'), may hold values from -0.21875 to 0.21875
- segment_level: int32 [16], P('mdl'), may hold values from 0 to 4, as said below
- dilate_rate: int32 [16], P('mdl'), may hold values from 1 to 8
- slide_length: int32 [1], replicated, may hold values from 8192 to 16384
Outputs:
- tile_embed: bfloat16 [256, 1536], P('enc')
- slide_out: bfloat16 [16384, 1536], P('enc', 'mdl')
Inputs may be any that keep to these rules, and one draw needn't show every extreme that they name: `tissue_index`: each row is a permutation. `segment_level`: each level from 0 to 4 belongs to three or more heads.
All inputs are finite; a program needn't handle non-finite values.
Results may differ from a plain program's by a relative error of at most 0.013.
Values may be sent and summed in bfloat16 or wider, within the bound.
A program may use at most 64 MiB of HBM per device.

v0:
```python
import jax
import jax.numpy as jnp
from jax import lax
from jax.sharding import PartitionSpec as P

HD = 48


def depthwise(tiles, kernel):
    side = tiles.shape[1]
    padded = jnp.pad(tiles.astype(jnp.float32), ((0, 0), (3, 3), (3, 3), (0, 0)))
    weight = kernel.astype(jnp.float32)
    total = jnp.zeros(tiles.shape, jnp.float32)
    for row in range(7):
        for col in range(7):
            total = total + padded[:, row : row + side, col : col + side, :] * weight[row, col]
    return total


def layer_norm(values, gain, epsilon):
    center = values - jnp.mean(values, axis=-1, keepdims=True)
    spread = jnp.mean(center * center, axis=-1, keepdims=True)
    return center * lax.rsqrt(spread + epsilon) * gain


def body(
    tile_feats,
    dw_weight,
    ln_gain,
    w_expand,
    w_contract,
    layer_scale,
    tile_owner,
    tissue_index,
    slide_embed,
    slide_gain,
    w_query,
    w_key,
    w_value,
    w_out,
    segment_level,
    dilate_rate,
    slide_length,
):
    tiles = tile_feats.shape[0]
    side = tile_feats.shape[1]
    width = tile_feats.shape[3]
    spots = side * side
    conv = depthwise(tile_feats, dw_weight)
    normed = layer_norm(conv, ln_gain, 1e-06).astype(jnp.bfloat16).reshape(tiles * spots, width)
    full_expand, full_contract = (
        lax.all_gather(w_expand, "enc", axis=0, tiled=True),
        lax.all_gather(w_contract, "enc", axis=0, tiled=True),
    )
    hidden = jax.nn.gelu(
        jnp.dot(normed, full_expand, preferred_element_type=jnp.float32), approximate=False
    ).astype(jnp.bfloat16)
    partial_rows = lax.dot_general(
        hidden, full_contract, (((1,), (1,)), ((), ())), preferred_element_type=jnp.float32
    )
    summed = lax.psum(partial_rows.astype(jnp.bfloat16), "mdl").astype(jnp.float32)
    mixed = summed.reshape(tiles, side, side, width)
    fresh = jnp.mean(tile_feats.astype(jnp.float32) + layer_scale * mixed, axis=(1, 2)).astype(
        jnp.bfloat16
    )
    me_enc = lax.axis_index("enc")
    strip_rows = slide_embed.shape[0]
    seq_total = strip_rows * lax.axis_size("enc")
    owners = tile_owner[:, 0]
    every_fresh, every_owner = (
        lax.all_gather(fresh, "enc", axis=0, tiled=True),
        lax.all_gather(owners.astype(jnp.bfloat16), "enc", axis=0, tiled=True),
    )
    slots = every_fresh.shape[0]
    tissue = tissue_index[0, :slots]
    row_ids = jnp.arange(strip_rows, dtype=jnp.int32)
    mine = every_owner.astype(jnp.int32) == me_enc
    hits = ((tissue[None, :] == row_ids[:, None]) & mine[None, :]).astype(jnp.float32)
    placed = jnp.dot(hits.astype(jnp.bfloat16), every_fresh, preferred_element_type=jnp.float32)
    covered = jnp.sum(hits, axis=1, keepdims=True) > 0.5
    strip = jnp.where(covered, placed, slide_embed.astype(jnp.float32)).astype(jnp.bfloat16)
    snorm = layer_norm(strip.astype(jnp.float32), slide_gain, 1e-05).astype(jnp.bfloat16)
    query = jnp.dot(snorm, w_query, preferred_element_type=jnp.float32).astype(jnp.bfloat16)
    key_local = jnp.dot(snorm, w_key, preferred_element_type=jnp.float32).astype(jnp.bfloat16)
    value_local = jnp.dot(snorm, w_value, preferred_element_type=jnp.float32).astype(jnp.bfloat16)
    heads_here = w_query.shape[1] // HD
    query = query.reshape(strip_rows, heads_here, HD)
    length = slide_length[0]
    scale = 1.0 / HD**0.5
    seg_len = jnp.right_shift(jnp.int32(seq_total), segment_level)
    q_index = me_enc * strip_rows + row_ids
    start_state = (
        jnp.full((heads_here, strip_rows), -1e30, jnp.float32),
        jnp.zeros((heads_here, strip_rows), jnp.float32),
        jnp.zeros((heads_here, strip_rows, HD), jnp.float32),
    )
    key_rows = lax.all_gather(key_local, "enc", axis=0, tiled=True)
    value_rows = lax.all_gather(value_local, "enc", axis=0, tiled=True)
    count = key_rows.shape[0]
    block = 512
    steps = count // block
    keys = key_rows.reshape(steps, block, heads_here, HD)
    values = value_rows.reshape(steps, block, heads_here, HD)
    firsts = jnp.arange(steps, dtype=jnp.int32) * block

    def step(state, inputs):
        top, total, acc = state
        k_block, v_block, first = inputs
        k_index = first + jnp.arange(block, dtype=jnp.int32)
        same_seg = (
            q_index[None, :, None] // seg_len[:, None, None]
            == k_index[None, None, :] // seg_len[:, None, None]
        )
        same_rate = (
            q_index[None, :, None] % dilate_rate[:, None, None]
            == k_index[None, None, :] % dilate_rate[:, None, None]
        )
        visible = same_seg & same_rate & (k_index[None, None, :] < length)
        scores = (
            jnp.einsum("qhd,khd->hqk", query, k_block, preferred_element_type=jnp.float32) * scale
        )
        scores = jnp.where(visible, scores, -1e30)
        new_top = jnp.maximum(top, jnp.max(scores, axis=2))
        weights = jnp.where(visible, jnp.exp(scores - new_top[:, :, None]), 0.0)
        shrink = jnp.exp(top - new_top)
        total = total * shrink + jnp.sum(weights, axis=2)
        acc = acc * shrink[:, :, None] + jnp.einsum(
            "hqk,khd->hqd",
            weights.astype(jnp.bfloat16),
            v_block,
            preferred_element_type=jnp.float32,
        )
        return ((new_top, total, acc), None)

    state, _ = lax.scan(step, start_state, (keys, values, firsts))
    top, total, acc = state
    live = (q_index < length)[None, :, None]
    attn = jnp.where(live, acc / jnp.where(total > 0, total, 1.0)[:, :, None], 0.0)
    attn = jnp.transpose(attn, (1, 0, 2)).reshape(strip_rows, heads_here * HD).astype(jnp.bfloat16)
    projected = jnp.dot(attn, w_out, preferred_element_type=jnp.float32)
    share = lax.psum_scatter(
        projected.astype(jnp.bfloat16), "mdl", scatter_dimension=1, tiled=True
    ).astype(jnp.float32)
    columns = share.shape[1]
    own_strip = lax.dynamic_slice_in_dim(strip, lax.axis_index("mdl") * columns, columns, 1)
    slide_out = (own_strip.astype(jnp.float32) + share).astype(jnp.bfloat16)
    return (fresh, slide_out)


def solution(mesh):
    placed = (
        P("enc", None, None, None),
        P(),
        P(),
        P("enc", "mdl"),
        P("enc", "mdl"),
        P(),
        P("enc", None),
        P("enc", None),
        P("enc", None),
        P(),
        P(None, "mdl"),
        P(None, "mdl"),
        P(None, "mdl"),
        P("mdl", None),
        P("mdl"),
        P("mdl"),
        P(),
    )
    return jax.shard_map(
        body,
        mesh=mesh,
        in_specs=placed,
        out_specs=(P("enc", None), P("enc", "mdl")),
        check_vma=False,
    )
```

profile of v0, /device:TPU:1, one launch (start us, length us, event | category | flops | bytes accessed | tf_op | source)
XLA Modules:
  0.0 807.6 jit_solution(14011169483488083247)
XLA Ops:
  13.7 10.6 %fusion.199 = (f32[4,8,8]{2,1,0:T(8,128)S(1)}, f32[4,8,8,1536]{3,2,1,0:T(8,128)S(1)}) fusion(f32[1536]{0:T(1024)S(1)} %get-tuple-element.375, f32[1536]{0:T(1024)S(1)} %get-tuple-element.376, f32[1536]{0:T(1024)S(1)} %get-tuple-element.377, f32[1536]{0:T(1024)S(1)} %get-tuple-element.378, f32[1536]{0:T(1024)S(1)} %get-tuple-element.379, ...), kind=kLoop, calls=%fused_computation.347 | loop fusion | flops 38534912 | bytes 3447808 | tf_op jit(solution)/shard_map/reduce_sum | solution.py:21
  25.3 74.6 %all-gather.9.cloned.1.call-done = bf16[1536,768]{1,0:T(8,128)(2,1)} async-done(((bf16[24,768]{1,0:T(8,128)(2,1)}), bf16[1536,768]{1,0:T(8,128)(2,1)}) %all-gather.9.cloned.1.call-update) | async-done | bytes 2359312 | tf_op jit(solution)/shard_map/all_gather | solution.py:53
  99.9 84.0 %all-gather.7.cloned.1.call-done = bf16[1536,768]{1,0:T(8,128)(2,1)} async-done(((bf16[24,768]{1,0:T(8,128)(2,1)}), bf16[1536,768]{1,0:T(8,128)(2,1)}) %all-gather.7.cloned.1.call-update) | async-done | bytes 2359312 | tf_op jit(solution)/shard_map/all_gather | solution.py:52
  183.9 6.6 convolution_convert_fusion
  190.9 123.8 %all-reduce.1 = bf16[256]{0:T(256)(128)(2,1)S(1)} all-reduce(bf16[256]{0:T(256)(128)(2,1)S(1)} %dynamic-update-slice), channel_id=2, replica_groups=mesh['enc'=64,'mdl'=8] {'enc'}, use_global_device_ids=true, to_apply=%add.1 | all-reduce | flops 256 | bytes 1024
  316.3 50.2 %all-gather.1 = bf16[64,4,1536]{2,1,0:T(4,128)(2,1)S(1)} all-gather(bf16[1,4,1536]{2,1,0:T(4,128)(2,1)S(1)} %fusion.217), channel_id=1, replica_groups=mesh['enc'=64,'mdl'=8] {'enc'}, dimensions={0}, use_global_device_ids=true | all-gather | bytes 798720 | tf_op jit(solution)/shard_map/all_gather | solution.py:71
  371.6 77.7 %all-gather.11.cloned.1.call-done = bf16[16384,96]{0,1:T(8,128)(2,1)} async-done(((bf16[256,96]{0,1:T(8,128)(2,1)}), bf16[16384,96]{0,1:T(8,128)(2,1)}) %all-gather.11.cloned.1.call-update) | async-done | bytes 3145744 | tf_op jit(solution)/shard_map/all_gather | solution.py:97
  449.3 3.1 copy.42
  452.4 3.5 copy.35
  455.9 76.2 %all-gather.13.cloned.1.call-done = bf16[16384,96]{0,1:T(8,128)(2,1)} async-done(((bf16[256,96]{0,1:T(8,128)(2,1)}), bf16[16384,96]{0,1:T(8,128)(2,1)}) %all-gather.13.cloned.1.call-update) | async-done | bytes 3145744 | tf_op jit(solution)/shard_map/all_gather | solution.py:98
  532.0 3.1 copy.43
  535.2 3.4 copy.36
  538.6 223.0 %while.20 = (s32[]{:T(128)}, f32[2,256]{1,0:T(2,128)S(1)}, f32[2,256]{1,0:T(2,128)S(1)}, f32[2,256,48]{1,2,0:T(8,128)S(1)}, s32[2,1,1]{0,2,1:T(1,128)S(1)}, /*in...) while((s32[]{:T(128)}, f32[2,256]{1,0:T(2,128)S(1)}, ...), condition=%wide.region_10.11_spmd.clone.clone.clone, body=%wide.region_7.10_spmd.clone.clone.clone.sunk | while | flops 55937292 | bytes 3684631 | solution.py:135
  541.9 1.6 fusion.230
  555.8 1.6 fusion.230
  569.8 1.6 fusion.230
  583.7 1.6 fusion.230
  597.6 1.6 fusion.230
  611.6 1.6 fusion.230
  625.5 1.6 fusion.230
  639.5 1.6 fusion.230
  653.4 1.6 fusion.230
  667.3 1.6 fusion.230
  763.6 35.3 %reduce-scatter.4.cloned.1.call-done = bf16[192,256]{1,0:T(8,128)(2,1)} async-done(((bf16[1536,256]{1,0:T(8,128)(2,1)}), bf16[192,256]{1,0:T(8,128)(2,1)}) %reduce-scatter.4.cloned.1.call-update) | async-done | bytes 98320
  (549 shorter events, 220.7 us)
Async XLA Ops:
  7.2 754.4 %copy-start = (bf16[96,1536]{1,0:T(8,128)(2,1)S(1)}, bf16[96,1536]{1,0:T(8,128)(2,1)}, u32[]{:S(2)}) copy-start(bf16[96,1536]{1,0:T(8,128)(2,1)} %param.32) | copy-start | bytes 884740
  7.2 92.8 %all-gather.9.cloned.1.call-start = ((), (), s32[]{:S(2)}) async-start(), calls=%async_computation.2 | async-start | bytes 2396160 | tf_op jit(solution)/shard_map/all_gather | solution.py:53
  7.9 176.0 %all-gather.7.cloned.1.call-start = ((), (), s32[]{:S(2)}) async-start(), calls=%async_computation.1 | async-start | bytes 2396160 | tf_op jit(solution)/shard_map/all_gather | solution.py:52
  8.7 306.2 %all-reduce.4.cloned.1.call-start = ((), (), s32[]{:S(2)}) async-start(), calls=%async_computation.3 | async-start | bytes 1572864 | tf_op jit(solution)/shard_map/psum | solution.py:61
  24.3 0.7 copy-start.5
  183.9 6.7 copy-start.10
  183.9 130.7 %copy-start.8 = (s32[1,256]{1,0:T(1,128)S(1)}, s32[1,256]{1,0:T(1,128)}, u32[]{:S(2)}) copy-start(s32[1,256]{1,0:T(1,128)} %param.26) | copy-start | bytes 3076
  183.9 130.9 %copy-start.1 = (bf16[4,8,8,1536]{3,2,1,0:T(8,128)(2,1)S(1)}, bf16[4,8,8,1536]{3,2,1,0:T(8,128)(2,1)}, u32[]{:S(2)}) copy-start(bf16[4,8,8,1536]{3,2,1,0:T(8,128)(2,1)} %param.19) | copy-start | bytes 2359300
  183.9 130.9 %copy-start.6 = (f32[1536]{0:T(1024)S(1)}, f32[1536]{0:T(1024)}, u32[]{:S(2)}) copy-start(f32[1536]{0:T(1024)} %param.24) | copy-start | bytes 18436
  190.6 258.8 %all-gather.11.cloned.1.call-start = ((), (), s32[]{:S(2)}) async-start(), calls=%async_computation.4 | async-start | bytes 3194880 | tf_op jit(solution)/shard_map/all_gather | solution.py:97
  316.3 50.4 %copy-start.9 = (bf16[256,1536]{1,0:T(8,128)(2,1)S(1)}, bf16[256,1536]{1,0:T(8,128)(2,1)}, u32[]{:S(2)}) copy-start(bf16[256,1536]{1,0:T(8,128)(2,1)} %param.27) | copy-start | bytes 2359300
  366.7 0.9 copy-start.7
  367.2 1.0 copy-start.2
  367.6 1.7 copy-start.3
  368.2 3.0 copy-start.11
  368.2 3.1 copy-start.4
  369.2 162.8 %all-gather.13.cloned.1.call-start = ((), (), s32[]{:S(2)}) async-start(), calls=%async_computation.5 | async-start | bytes 3194880 | tf_op jit(solution)/shard_map/all_gather | solution.py:98
  370.3 428.6 %reduce-scatter.4.cloned.1.call-start = ((), (), s32[]{:S(2)}) async-start(), calls=%async_computation.6 | async-start | bytes 884736
  535.2 3.4 copy-start.12
Sparse Core Ops, SparseCore 0:
  11.3 88.6 all-gather.8
  103.2 80.6 all-gather.6
  190.7 74.0 all-reduce.3
  369.3 79.9 all-gather.10
  452.9 79.1 all-gather.12
  763.1 35.7 reduce-scatter.3
where the time goes:
time: 815 us; the launch traced here: 808 us
  waiting for transfers between devices  349 us (43%)
  blocking collectives  174 us (21%)
  other arithmetic  121 us (15%)
  matrix products  107 us (13%)
  local copies, waits for them, and re-layouts  36.9 us (5%)
  between operations  15.8 us (2%)
    unnamed x1, blocking collectives  124 us
    all_gather x1, waiting for transfers between devices, body(): lax.all_gather(w_expand, 'enc', axis=0, tiled=True)  84 us
    all_gather x1, waiting for transfers between devices, body(): key_rows = lax.all_gather(key_local, 'enc', axis=0, tiled=True)  77.7 us
    all_gather x1, waiting for transfers between devices, body(): value_rows = lax.all_gather(value_local, 'enc', axis=0, tiled=True)  76.2 us
    all_gather x1, waiting for transfers between devices, body(): lax.all_gather(w_contract, 'enc', axis=0, tiled=True)  74.6 us
    dot_general x32, matrix products, step(): jnp.einsum('qhd,khd->hqk', query, k_block, preferred_element_type=jnp.flo...  50.2 us
    all_gather x1, blocking collectives, body(): lax.all_gather(fresh, 'enc', axis=0, tiled=True)  50.2 us
    dot_general x32, matrix products, step(): jnp.einsum('hqk,khd->hqd', weights.astype(jnp.bfloat16), v_block, preferr...  46.2 us
  transfers between devices with their start and end apart: 6, of which 5 were waited for; matrix products, arithmetic and copies ran while one was open for 3% of the time, Pallas kernels for 0%

commit v1 on v0

v1 whole, which is shorter than its diff:
```python
import functools
import math

import jax
import jax.numpy as jnp
from jax import lax
from jax.experimental import pallas as pl
from jax.experimental.pallas import tpu as pltpu
from jax.sharding import PartitionSpec as P

MESH = pl.DeviceIdType.MESH
F32 = jnp.float32
BF16 = jnp.bfloat16
HD = 48
D = 1536
NEG = -1e30
NY, NX, NZ = 8, 4, 8


def wrap(v, n):
    return lax.rem(v + 2 * n, n)


def place():
    e = lax.axis_index("enc")
    m = lax.axis_index("mdl")
    return e, m, lax.rem(e, 2), lax.rem(e // 2, NX), e // (2 * NX)


def device(y, x, c, m):
    return (y * (2 * NX) + x * 2 + c, m)


class Gather:
    def __init__(self, wave, buf, sems, split, share):
        self.w, self.buf, self.split, self.share = wave, buf, split, share
        self.send, self.recv, self.dsend, self.drecv = sems
        self.e, self.m, self.c, self.x, self.y = place()

    def half(self, core, y, x, h):
        ref = self.at(core, y, x)
        if self.split is None:
            return ref if h == 0 else None
        rows = self.buf.shape[3]
        return ref.at[pl.ds(0, self.split)] if h == 0 else ref.at[pl.ds(self.split, rows - self.split)]

    def at(self, core, y, x):
        return self.buf.at[core if self.share else 0, y, x]

    def own(self):
        return (self.c if self.share else 0, self.y, self.x)

    def pieces(self, core, s):
        x, y, m = self.x, self.y, self.m
        out = []
        for d, sg in ((0, 1), (1, -1)):
            wx = lambda k: wrap(x - k * sg, NX)
            wy = lambda k: wrap(y - k * sg, NY)
            if core == 0:
                if s < 2:
                    to = device(y, wx(-1), 0, m)
                    if s == 0:
                        p, q = self.at(0, y, x), self.at(0, y, wx(1))
                    else:
                        p, q = self.half(0, y, wx(1), d), self.half(0, y, wx(2), d)
                else:
                    k = s - 2
                    to = device(wy(-1), x, 0, m)
                    if k < 3:
                        p, q = self.at(0, wy(k), pl.ds(0, 4)), self.at(0, wy(k + 1), pl.ds(0, 4))
                    else:
                        p, q = self.at(0, wy(k), pl.ds(2 * d, 2)), self.at(0, wy(k + 1), pl.ds(2 * d, 2))
            else:
                if s < 4:
                    to = device(wy(-1), x, 1, m)
                    if s < 3:
                        p, q = self.at(1, wy(s), x), self.at(1, wy(s + 1), x)
                    else:
                        p, q = self.half(1, wy(s), x, d), self.half(1, wy(s + 1), x, d)
                else:
                    k = s - 4
                    to = device(y, wx(-1), 1, m)
                    if k < 1:
                        p, q = self.at(1, pl.ds(0, 8), x), self.at(1, pl.ds(0, 8), wx(1))
                    else:
                        p, q = self.at(1, pl.ds(4 * d, 4), wx(1)), self.at(1, pl.ds(4 * d, 4), wx(2))
            if p is not None:
                out.append((d, p, q, to))
        return out

    def remote(self, ref, s, d, to):
        return pltpu.make_async_remote_copy(
            src_ref=ref, dst_ref=ref, send_sem=self.send.at[self.w, s, d], recv_sem=self.recv.at[self.w, s, d],
            device_id=to, device_id_type=MESH)

    def shared(self, core):
        x, y = self.x, self.y
        if core == 0:
            b = lambda k: self.at(0, wrap(y + k, NY), pl.ds(0, 4))
            return {2: [b(0)], 3: [b(-1), b(1)], 4: [b(-2), b(2)], 5: [b(-3), b(3)], 6: [b(4)]}
        b = lambda k: self.at(1, pl.ds(0, 8), wrap(x + k, NX))
        return {4: [b(0)], 5: [b(-1), b(1)], 6: [b(2)]}

    def share_copies(self, core):
        to = device(self.y, self.x, 1 - core, self.m)
        out, k = {}, 0
        for s, refs in self.shared(core).items():
            out[s] = []
            for ref in refs:
                out[s].append(pltpu.make_async_remote_copy(
                    src_ref=ref, dst_ref=ref, send_sem=self.dsend.at[self.w, k], recv_sem=self.drecv.at[self.w, k],
                    device_id=to, device_id_type=MESH))
                k += 1
        return out

    def step(self, s):
        for core in (0, 1):

            @pl.when(self.c == core)
            def _():
                if s > 0:
                    for d, _, q, to in self.pieces(core, s - 1):
                        self.remote(q, s - 1, d, to).wait_recv()
                if s < 6:
                    for d, p, _, to in self.pieces(core, s):
                        self.remote(p, s, d, to).start()
                if self.share:
                    for copy in self.share_copies(core).get(s, []):
                        copy.start()

    def drain(self):
        for core in (0, 1):

            @pl.when(self.c == core)
            def _():
                for s in range(6):
                    for d, p, _, to in self.pieces(core, s):
                        self.remote(p, s, d, to).wait_send()
                if self.share:
                    for copies in self.share_copies(core).values():
                        for copy in copies:
                            copy.wait_send()
                    for copies in self.share_copies(1 - core).values():
                        for copy in copies:
                            copy.wait_recv()


def z_copies(src, dst, send, recv, first):
    e, m, _, _, _ = place()
    out = []
    for j in range(1, NZ):
        to, back = wrap(m + j, NZ), wrap(m - j, NZ)
        mk = lambda s, d: pltpu.make_async_remote_copy(
            src_ref=s, dst_ref=d, send_sem=send.at[first + j - 1], recv_sem=recv.at[first + j - 1],
            device_id=(e, to), device_id_type=MESH)
        out.append((mk(src(to), dst.at[m]), mk(src(to), dst.at[back])))
    return out


def greet(targets):
    barrier = pltpu.get_barrier_semaphore()
    for to in targets:
        pl.semaphore_signal(barrier, inc=1, device_id=to, device_id_type=MESH)
    pl.semaphore_wait(barrier, len(targets))


def normed_rows(values, gain, epsilon):
    center = values - jnp.mean(values, axis=-1, keepdims=True)
    spread = jnp.mean(center * center, axis=-1, keepdims=True)
    return center * lax.rsqrt(spread + epsilon) * gain


def encode(feats, dw, lng, we, wc, ls, own, tissue, slide, sg, wk, wv, wo,
           emb, kvb, metab, fb, wor,
           wxs, wxr, wb, wcb, nb, conv, mf, dxs, dxr, zs, zr, exs, exr, ws,
           send, recv, dsend, drecv, msend, mrecv):
    e, m, c, x, y = place()
    other = device(y, x, 1 - c, m)
    targets = [other]
    for sg_ in (1, -1):
        targets.append(device(y, wrap(x + sg_, NX), c, m))
        targets.append(device(wrap(y + sg_, NY), x, c, m))
    for j in range(1, NZ):
        targets.append((e, wrap(m + j, NZ)))
    greet(targets)
    sems = (send, recv, dsend, drecv)

    def across(src, dst, k):
        return pltpu.make_async_remote_copy(
            src_ref=src, dst_ref=dst, send_sem=msend.at[k], recv_sem=mrecv.at[k], device_id=other, device_id_type=MESH)

    for core in (0, 1):

        @pl.when(c == core)
        def _():
            lanes = pl.ds(384 * (1 - core), 384)
            wxs[0] = we[:, lanes].astype(F32)
            wxs[1] = wc[:, lanes].astype(F32)

    cross_w = across(wxs, wxr, 0)
    cross_w.start()

    snorm = normed_rows(slide[...].astype(F32), sg[...], 1e-05).astype(BF16)
    g_kv = Gather(2, kvb, sems, 96, True)
    for i, ref in enumerate((wk, wv)):
        rows = jnp.dot(snorm, ref[...], preferred_element_type=F32)
        kvb[c, y, x, pl.ds(96 * i, 96), :] = rows.T.astype(BF16)

    g_meta = Gather(3, metab, sems, None, True)
    row = lax.broadcasted_iota(jnp.int32, (16, 128), 0)
    lane = lax.broadcasted_iota(jnp.int32, (16, 128), 1)
    info = jnp.where(row == 0, tissue[:, pl.ds(0, 128)].astype(F32), 0.0)
    info = jnp.where(row == 1, tissue[:, pl.ds(128, 128)].astype(F32), info)
    for i in range(4):
        info = jnp.where((row - 2) * 128 + lane == 4 * e + i, own[i, 0].astype(F32), info)
    metab[c, y, x] = info.astype(BF16)

    cross_w.wait()
    g_w = Gather(0, wb, sems, 16, False)
    g_wc = Gather(1, wcb, sems, 32, False)
    for core in (0, 1):

        @pl.when(c == core)
        def _():
            lanes = pl.ds(384 * core, 384)
            for k, (src, dst) in enumerate(((we, wb), (wc, wcb))):
                mine = src[:, lanes].astype(F32)
                pair = [mine, wxr[k]] if core == 0 else [wxr[k], mine]
                dst[0, y, x] = jnp.concatenate(pair, axis=0).astype(BF16)

    g_w.step(0)
    g_wc.step(0)
    g_kv.step(0)
    g_meta.step(0)

    for j in range(NZ):
        ws[j] = wo[:, 192 * j:192 * j + 192]
    wor[m] = ws[m]
    wo_copies = z_copies(lambda to: ws.at[to], wor, msend, mrecv, 16)
    for copy, _ in wo_copies:
        copy.start()

    sub = lax.broadcasted_iota(jnp.int32, (8, 8, 128), 1)

    def conv_tile(t):
        def chunk(k, carry):
            lanes = pl.ds(pl.multiple_of(k * 128, 128), 128)
            xs = feats[t, :, :, lanes].astype(F32)
            mf[pl.ds(t, 1), lanes] = jnp.sum(jnp.sum(xs, axis=0), axis=0, keepdims=True)
            weight = dw[:, :, lanes].astype(F32)
            total = [jnp.zeros((8, 128), F32)] * 8
            for col in range(7):
                off = col - 3
                if off == 0:
                    moved = xs
                else:
                    moved = pltpu.roll(xs, (-off) % 8, axis=1)
                    moved = jnp.where((sub + off >= 0) & (sub + off < 8), moved, 0.0)
                for r in range(7):
                    tap = weight[r, col:col + 1, :]
                    for h in range(8):
                        if 0 <= h + r - 3 < 8:
                            total[h] = total[h] + moved[h + r - 3] * tap
            for h in range(8):
                conv[pl.ds(8 * h, 8), lanes] = total[h]
            return carry

        lax.fori_loop(0, D // 128, chunk, 0)
        nb[c, pl.ds(64 * t, 64), :] = normed_rows(conv[...], lng[...], 1e-06).astype(BF16)

    def cross_n(t):
        ref = nb.at[c, pl.ds(64 * t, 64)]
        return across(ref, ref, 1 + t)

    for t in range(4):
        conv_tile(t)
        cross_n(t).start()
        for g in (g_w, g_wc):
            g.step(t + 1)
        if t < 2:
            g_kv.step(t + 1)
            g_meta.step(t + 1)
    for s in (5, 6):
        g_w.step(s)
        g_wc.step(s)
    for s in (3,):
        g_kv.step(s)
        g_meta.step(s)

    for t in range(4):
        cross_n(t).wait_send()
        ref = nb.at[1 - c, pl.ds(64 * t, 64)]
        across(ref, ref, 1 + t).wait_recv()

    sums = []
    wfull = wb[0].reshape(D, 384)
    for k in range(4):
        pre = jnp.dot(nb[k // 2, pl.ds(128 * (k % 2), 128), :], wfull, preferred_element_type=F32)
        act = (0.5 * pre * (1.0 + lax.erf(pre * (0.5 ** 0.5)))).astype(BF16).astype(F32)
        for i in range(2):
            sums.append(jnp.sum(act[64 * i:64 * i + 64], axis=0, keepdims=True))
    hsum = jnp.concatenate(sums, axis=0)
    high = hsum.astype(BF16)
    low = (hsum - high.astype(F32)).astype(BF16)
    part = lax.dot_general(high, wcb[0].reshape(D, 384), (((1,), (1,)), ((), ())), preferred_element_type=F32)
    part += lax.dot_general(low, wcb[0].reshape(D, 384), (((1,), (1,)), ((), ())), preferred_element_type=F32)
    part = part * (ls[...] * (1.0 / 64.0))
    mine = mf[...] * (1.0 / 512.0)
    for core in (0, 1):

        @pl.when(c == core)
        def _():
            blank = jnp.zeros((4, D), F32)
            both = part + jnp.concatenate([mine, blank] if core == 0 else [blank, mine], axis=0)
            zs[...] = both[:, 768 * core:768 * core + 768]
            dxs[...] = both[:, 768 * (1 - core):768 * (1 - core) + 768]

    cross_p = across(dxs, dxr, 5)
    cross_p.start()
    g_kv.step(4)
    g_meta.step(4)
    cross_p.wait()
    zs[...] = zs[...] + dxr[...]
    zr[m] = zs[...]
    zc = z_copies(lambda to: zs, zr, msend, mrecv, 8)
    for copy, _ in zc:
        copy.start()
    g_kv.step(5)
    g_meta.step(5)
    for copy, back in zc:
        copy.wait_send()
        back.wait_recv()
    fresh = jnp.sum(zr[...], axis=0)
    exs[...] = fresh
    cross_e = across(exs, exr, 6)
    cross_e.start()
    fb[c, y, x] = jnp.concatenate([fresh[:, :384], fresh[:, 384:]], axis=0).astype(BF16)
    g_f = Gather(4, fb, sems, None, True)
    g_f.step(0)
    g_kv.step(6)
    g_meta.step(6)
    for s in range(1, 7):
        g_f.step(s)
    cross_e.wait()
    for core in (0, 1):

        @pl.when(c == core)
        def _():
            rows = pl.ds(4 * core, 4)
            emb[:, pl.ds(768 * core, 768)] = exs[rows, :].astype(BF16)
            emb[:, pl.ds(768 * (1 - core), 768)] = exr[rows, :].astype(BF16)

    for copy, back in wo_copies:
        copy.wait_send()
        back.wait_recv()
    for g in (g_w, g_wc, g_kv, g_meta, g_f):
        g.drain()


def attend(level, rate, length, place_ref, kvb, metab, fb, tissue, slide, sg, wq, wk, wv, attn, own_cols, fresh_ref, code_ref):
    e, m = place_ref[0], place_ref[1]
    seq = 16384
    n = length[0]
    for c in range(2):
        for h in range(2):
            lanes = pl.ds(768 * c + 384 * h, 384)
            block = fb[c].reshape(32, 16, 384).astype(F32)[:, 8 * h:8 * h + 8, :]
            fresh_ref[:, lanes] = block.reshape(256, 384).astype(BF16)
    fresh = fresh_ref[...]

    info = [metab[c].reshape(32, 16, 128).astype(F32) for c in range(2)]
    owner = jnp.concatenate([sum(jnp.sum(i[:, 2 + k, :], axis=0, keepdims=True) for i in info) for k in range(2)], axis=1)
    strip_of = 2 * lax.broadcasted_iota(jnp.int32, (32, 256), 0)
    picks, spots = [], 0.0
    for c in range(2):
        rows = jnp.concatenate([info[c][:, 0, :], info[c][:, 1, :]], axis=1)
        pick = ((strip_of + c).astype(F32) == owner).astype(F32)
        picks.append(pick.astype(BF16))
        spots = spots + jnp.sum(pick * rows, axis=0, keepdims=True)
    row_id = lax.broadcasted_iota(jnp.int32, (256, 256), 0).astype(F32)
    at_row = row_id == spots
    at_row_bf = at_row.astype(F32).astype(BF16)
    gone = [lax.dot_general(p, at_row_bf, (((1,), (1,)), ((), ())), preferred_element_type=F32) for p in picks]
    code_ref[0] = gone[0]
    code_ref[1] = gone[1]

    hits = (at_row & (owner == e.astype(F32))).astype(F32)
    covered = jnp.sum(hits, axis=1, keepdims=True) > 0.5
    placed = jnp.dot(hits.astype(BF16), fresh, preferred_element_type=F32)
    strip = jnp.where(covered, placed, slide[...].astype(F32))
    for j in range(NZ):

        @pl.when(m == j)
        def _():
            own_cols[...] = strip[:, 192 * j:192 * j + 192].astype(BF16)

    snorm = normed_rows(strip, sg[...], 1e-05).astype(BF16)
    query = jnp.dot(snorm, wq[...], preferred_element_type=F32).astype(BF16)
    fnorm = normed_rows(fresh.astype(F32), sg[...], 1e-05).astype(BF16)
    fkey = jnp.dot(fnorm, wk[...], preferred_element_type=F32).T.astype(BF16)
    fval = jnp.dot(fnorm, wv[...], preferred_element_type=F32).T.astype(BF16)

    feat = lax.broadcasted_iota(jnp.int32, (32, 256), 0)
    qfeat = lax.broadcasted_iota(jnp.int32, (256, 32), 1)
    lane = lax.broadcasted_iota(jnp.int32, (1, 256), 1).astype(F32)
    qrow = lax.broadcasted_iota(jnp.int32, (256, 1), 0) + e * 256
    c2 = HD ** -0.5 * math.log2(math.e)
    for h in range(2):
        r = rate[h].astype(F32)
        shift = 14 - level[h]
        width = jnp.left_shift(jnp.int32(1), shift).astype(F32)

        def classes(pos):
            seg = jnp.floor((pos + 0.5) / width)
            res = pos - r * jnp.floor((pos + 0.5) / r)
            return res, seg

        qres, qseg = classes(qrow.astype(F32))
        qhot = ((qfeat < 8) & (qfeat.astype(F32) == qres)) | ((qfeat >= 8) & (qfeat < 24) & ((qfeat - 8).astype(F32) == qseg)) | (qfeat == 24)
        qaug = jnp.concatenate([query[:, HD * h:HD * h + HD].astype(F32), jnp.where(qhot, NEG, 0.0)], axis=1).astype(BF16)

        def features(pos, dead):
            res, seg = classes(pos)
            miss = jnp.where(feat < 8, (feat.astype(F32) != res).astype(F32), ((feat - 8).astype(F32) != seg).astype(F32))
            gone = jnp.where((pos >= n.astype(F32)) | (dead > 0.5), 1.0, 0.0)
            miss = jnp.where(feat == 24, gone, miss)
            return jnp.where(feat > 24, 0.0, miss).astype(BF16)

        def update(state, keys, vals):
            top, acc = state
            s = jnp.dot(qaug, keys, preferred_element_type=F32)
            new = jnp.maximum(top, jnp.max(s, axis=1, keepdims=True))
            p = jnp.exp2(s * c2 - new * c2).astype(BF16)
            acc = acc * jnp.exp2((top - new) * c2) + lax.dot_general(p, vals, (((1,), (1,)), ((), ())), preferred_element_type=F32)
            return new, acc

        def augmented(k, f):
            return jnp.concatenate([k, f], axis=0)

        def with_ones(v):
            return jnp.concatenate([v, jnp.ones((16, v.shape[1]), BF16)], axis=0)

        fpos = owner * 256.0 + spots
        state = (jnp.full((256, 1), NEG, F32), jnp.zeros((256, 64), F32))
        state = update(state, augmented(fkey[HD * h:HD * h + HD], features(fpos, jnp.zeros((1, 256), F32))),
                       with_ones(fval[HD * h:HD * h + HD]))

        def group(g, state):
            keys, vals = [], []
            for i in range(4):
                s = 4 * g + i
                chip = 2 * g + i // 2
                ref = kvb.at[i % 2, chip // NX, lax.rem(chip, NX)]
                dead = code_ref[i % 2, pl.ds(chip, 1), :]
                pos = lane + (s * 256).astype(F32)
                keys.append(augmented(ref[pl.ds(HD * h, HD), :], features(pos, dead)))
                vals.append(with_ones(ref[pl.ds(96 + HD * h, HD), :]))
            return update(state, jnp.concatenate(keys, axis=1), jnp.concatenate(vals, axis=1))

        groups = jnp.right_shift(jnp.int32(16), level[h])
        first = e // 4 // groups * groups
        last = jnp.minimum(first + groups, (n + 1023) // 1024)
        top, acc = lax.fori_loop(first, last, group, state)
        total = acc[:, HD:HD + 1]
        out = acc[:, :HD] / jnp.where(total > 0, total, 1.0)
        out = jnp.where(qrow < n, out, 0.0)
        attn[pl.ds(HD * h, HD), :] = out.T.astype(BF16)


def project(attn, wor, own_cols, out, ab, msend, mrecv):
    e, m, c, x, y = place()
    greet([(e, wrap(m + j, NZ)) for j in range(1, NZ)])
    ab[m] = attn[...]
    copies = z_copies(lambda to: attn, ab, msend, mrecv, 0)
    for copy, _ in copies:
        copy.start()
    for copy, back in copies:
        copy.wait_send()
        back.wait_recv()
    total = lax.dot_general(ab[...].reshape(768, 256), wor[...].reshape(768, 192), (((0,), (0,)), ((), ())), preferred_element_type=F32)
    out[...] = (own_cols[...].astype(F32) + total).astype(BF16)


VM = pl.BlockSpec(memory_space=pltpu.VMEM)
SM = pl.BlockSpec(memory_space=pltpu.SMEM)


def shape(dims, dtype=BF16):
    return jax.ShapeDtypeStruct(dims, dtype)


def body(tile_feats, dw_weight, ln_gain, w_expand, w_contract, layer_scale, tile_owner, tissue_index, slide_embed,
         slide_gain, w_query, w_key, w_value, w_out, segment_level, dilate_rate, slide_length):
    dma = pltpu.SemaphoreType.DMA
    lng, ls, sg = ln_gain.reshape(1, D), layer_scale.reshape(1, D), slide_gain.reshape(1, D)
    emb, kvb, metab, fb, wor = pl.pallas_call(
        encode,
        out_shape=[shape((4, D)), shape((2, 8, 4, 192, 256)), shape((2, 8, 4, 16, 128)), shape((2, 8, 4, 16, 384)), shape((8, 96, 192))],
        in_specs=[VM] * 6 + [SM] + [VM] * 6,
        out_specs=[VM] * 5,
        scratch_shapes=[
            pltpu.VMEM((2, 24, 384), F32), pltpu.VMEM((2, 24, 384), F32),
            pltpu.VMEM((1, 8, 4, 48, 384), BF16), pltpu.VMEM((1, 8, 4, 48, 384), BF16),
            pltpu.VMEM((2, 256, D), BF16), pltpu.VMEM((64, D), F32), pltpu.VMEM((4, D), F32),
            pltpu.VMEM((8, 768), F32), pltpu.VMEM((8, 768), F32), pltpu.VMEM((8, 768), F32), pltpu.VMEM((8, 8, 768), F32),
            pltpu.VMEM((8, 768), F32), pltpu.VMEM((8, 768), F32), pltpu.VMEM((8, 96, 192), BF16),
            dma((5, 6, 2)), dma((5, 6, 2)), dma((5, 8)), dma((5, 8)), dma((24,)), dma((24,)),
        ],
        name="encode",
        compiler_params=pltpu.CompilerParams(collective_id=0, has_side_effects=True, vmem_limit_bytes=48 * 2**20),
    )(tile_feats, dw_weight, lng, w_expand, w_contract, ls, tile_owner, tissue_index, slide_embed, sg, w_key, w_value, w_out)
    here = jnp.stack([lax.axis_index("enc"), lax.axis_index("mdl")]).astype(jnp.int32)
    attn, own_cols = pl.pallas_call(
        attend,
        out_shape=[shape((96, 256)), shape((256, 192))],
        in_specs=[SM] * 4 + [VM] * 9,
        out_specs=[VM] * 2,
        scratch_shapes=[pltpu.VMEM((256, D), BF16), pltpu.VMEM((2, 32, 256), F32)],
        name="attend",
        compiler_params=pltpu.CompilerParams(vmem_limit_bytes=48 * 2**20),
    )(segment_level, dilate_rate, slide_length, here, kvb, metab, fb, tissue_index, slide_embed, sg, w_query, w_key, w_value)
    slide_out = pl.pallas_call(
        project,
        out_shape=shape((256, 192)),
        in_specs=[VM] * 3,
        out_specs=VM,
        scratch_shapes=[pltpu.VMEM((8, 96, 256), BF16), dma((7,)), dma((7,))],
        name="project",
        compiler_params=pltpu.CompilerParams(collective_id=1, has_side_effects=True, vmem_limit_bytes=32 * 2**20),
    )(attn, wor, own_cols)
    return emb, slide_out


def solution(mesh):
    placed = (
        P("enc", None, None, None),
        P(),
        P(),
        P("enc", "mdl"),
        P("enc", "mdl"),
        P(),
        P("enc", None),
        P("enc", None),
        P("enc", None),
        P(),
        P(None, "mdl"),
        P(None, "mdl"),
        P(None, "mdl"),
        P("mdl", None),
        P("mdl"),
        P("mdl"),
        P(),
    )
    return jax.shard_map(
        body,
        mesh=mesh,
        in_specs=placed,
        out_specs=(P("enc", None), P("enc", "mdl")),
        check_vma=False,
    )
```

time: 815 us -> 150 us (0.18)
  waiting for transfers between devices: 349 us -> 0 us
  blocking collectives: 174 us -> 0 us
  Pallas kernels: 0 us -> 131 us
  other arithmetic: 121 us -> 0.08 us
  matrix products: 107 us -> 0 us
  local copies, waits for them, and re-layouts: 36.9 us -> 16.5 us
  between operations: 15.8 us -> 1.36 us
    all_gather x4 -> x0, waiting for transfers between devices: 312 us -> none  [the longest x1 84 us: body(): lax.all_gather(w_expand, 'enc', axis=0, tiled=True)]
    pallas_call x0 -> x3, Pallas kernels: none -> 131 us  [the longest x1 90.4 us: body(): pl.pallas_call(encode, out_shape=[shape((4, D)), shape((2, 8, 4, 192, 256...]
    unnamed x1 -> x0, blocking collectives: 124 us -> none
    dot_general x70 -> x0, matrix products: 107 us -> none  [the longest x32 50.2 us: step(): jnp.einsum('qhd,khd->hqk', query, k_block, preferred_element_type=jnp.flo...]
    all_gather x1 -> x0, blocking collectives: 50.2 us -> none  [body(): lax.all_gather(fresh, 'enc', axis=0, tiled=True)]
    lt x65 -> x0, other arithmetic: 41.7 us -> none  [the longest x32 41.5 us: step(): visible = same_seg & same_rate & (k_index[None, None, :] < length)]
    unnamed x7 -> x0, waiting for transfers between devices: 36.8 us -> none
    reduce_sum x37 -> x0, other arithmetic: 30.5 us -> none  [the longest x32 17.7 us: step(): total = total * shrink + jnp.sum(weights, axis=2)]
  transfers between devices with their start and end apart: 6 -> 0, of which waited for: 5 -> 0; matrix products, arithmetic and copies ran while one was open for 3% -> 0% of each run, Pallas kernels for 0% -> 0%
where the time goes in v1:
time: 150 us; the launch traced here: 149 us
  Pallas kernels  131 us (87%)
  local copies, waits for them, and re-layouts  16.5 us (11%)
    pallas_call x1, Pallas kernels, body(): pl.pallas_call(encode, out_shape=[shape((4, D)), shape((2, 8, 4, 192, 256...  90.4 us
    pallas_call x1, Pallas kernels, body(): pl.pallas_call(project, out_shape=shape((256, 192)), in_specs=[VM] * 3, o...  29.1 us
    unnamed x26, local copies, waits for them, and re-layouts  14.4 us
    pallas_call x1, Pallas kernels, body(): pl.pallas_call(attend, out_shape=[shape((96, 256)), shape((256, 192))], i...  11.6 us

profile of v1, /device:TPU:1, one launch (start us, length us, event | category | flops | bytes accessed | tf_op | source)
XLA Modules:
  0.0 149.1 jit_solution(4997275533348976770)
XLA Ops:
  1.3 0.1 pad_add_fusion.place_ref
  1.4 0.7 copy.19.own
  2.1 0.7 reshape.15.sg
  2.8 0.7 reshape.13.lng
  3.5 0.7 reshape.14.ls
  4.2 1.2 copy.20.wk
  5.4 1.2 copy.21.wv
  6.6 1.2 copy.22.wq
  7.8 0.0 copy-start
  7.8 1.1 copy-done
  8.9 1.1 copy-done.2
  10.1 1.0 copy-done.3
  11.0 0.9 copy-done.4
  11.9 0.8 copy-done.5
  12.7 0.8 copy-done.6
  13.5 0.7 copy-done.7
  14.1 90.4 %encode.1 = (bf16[4,1536]{1,0:T(4,128)(2,1)S(1)}, bf16[2,8,4,192,256]{4,3,2,1,0:T(8,128)(2,1)}, bf16[2,8,4,16,128]{4,3,2,1,0:T(8,128)(2,1)S(1)}, bf16[2,8,4,16,3...) custom-call(bf16[4,8,8,1536]{3,2,1,0:T(8,128)(2,1)S(1)} %copy-done.2, bf16[7,7,1536]{2,1,0:T(8,128)(2,1)S(1)} %copy-done.4, ...), custom_call_target="tpu_custom_call" | custom-call | tf_op jit(solution)/shard_map/encode/pallas_call | solution.py:496
  104.6 1.1 copy-done.1
  105.7 0.7 copy-done.8
  106.3 0.7 copy-done.9
  107.0 11.6 %attend.1 = (bf16[96,256]{1,0:T(8,128)(2,1)S(1)}, bf16[256,192]{1,0:T(8,128)(2,1)S(1)}) custom-call(s32[2]{0:T(128)S(1)} %copy-done.8, s32[2]{0:T(128)S(1)} %copy-done.9, s32[1]{0:T(128)S(6)} %copy.27.length, s32[2]{0:T(128)S(1)} %pad_add_fusion.place_ref, bf16[2,8,4,192,256]{4,3,2,1,0:T(8,128)(2,1)} %get-tuple-element.10.kvb, ...), custom_call_target="tpu_custom_call" | custom-call | tf_op jit(solution)/shard_map/attend/pallas_call | solution.py:513
  118.6 29.1 %project.1 = bf16[256,192]{1,0:T(8,128)(2,1)S(1)} custom-call(bf16[96,256]{1,0:T(8,128)(2,1)S(1)} %get-tuple-element.13.attn, bf16[8,96,192]{2,1,0:T(8,128)(2,1)S(1)} %get-tuple-element.14.wor, bf16[256,192]{1,0:T(8,128)(2,1)S(1)} %get-tuple-element.15.own_cols), custom_call_target="tpu_custom_call" | custom-call | tf_op jit(solution)/shard_map/project/pallas_call | solution.py:522
  147.7 0.7 copy.25
  148.5 0.6 copy.28
  (9 shorter events, 0.0 us)
Async XLA Ops:
  7.8 1.1 copy-start
  8.9 1.1 copy-start.2
  10.0 1.0 copy-start.3
  11.0 0.9 copy-start.4
  11.9 0.8 copy-start.5
  12.7 0.8 copy-start.6
  13.5 0.7 copy-start.7
  104.5 1.1 copy-start.1
  105.7 0.7 copy-start.8
  106.3 0.7 copy-start.9

commit v2 on v1

v2 whole, which is shorter than its diff:
```python
import functools
import math

import jax
import jax.numpy as jnp
from jax import lax
from jax.experimental import pallas as pl
from jax.experimental.pallas import tpu as pltpu
from jax.sharding import PartitionSpec as P

MESH = pl.DeviceIdType.MESH
F32 = jnp.float32
BF16 = jnp.bfloat16
HD = 48
D = 1536
NEG = -1e30
NY, NX, NZ = 8, 4, 8


def wrap(v, n):
    return lax.rem(v + 2 * n, n)


def place():
    e = lax.axis_index("enc")
    m = lax.axis_index("mdl")
    return e, m, lax.rem(e, 2), lax.rem(e // 2, NX), e // (2 * NX)


def device(y, x, c, m):
    return (y * (2 * NX) + x * 2 + c, m)


class Gather:
    def __init__(self, wave, buf, sems, orders, direct, split=None, share=""):
        self.w, self.buf, self.orders, self.direct, self.split, self.share = wave, buf, orders, direct, split, share
        self.send, self.recv, self.dsend, self.drecv = sems
        self.e, self.m, self.c, self.x, self.y = place()

    def at(self, core, y, x):
        return self.buf.at[core if self.share else 0, y, x]

    def own(self):
        return (self.c if self.share else 0, self.y, self.x)

    def plan(self, core):
        first, second = self.orders[core]
        size = {"x": NX, "y": NY}
        n1, n2 = size[first], size[second]

        def go(axis, k):
            if axis == "x":
                return device(self.y, wrap(self.x + k, NX), core, self.m)
            return device(wrap(self.y + k, NY), self.x, core, self.m)

        p1, p2 = (self.x, self.y) if first == "x" else (self.y, self.x)

        def ref(i1, i2):
            return self.at(core, i2, i1) if first == "x" else self.at(core, i1, i2)

        steps = []
        if self.direct[core][0]:
            steps.append([(k - 1, ref(p1, p2), ref(wrap(p1 - k, n1), p2), go(first, k)) for k in range(1, n1)])
        else:
            for s in range(n1 // 2):
                step = []
                for d, sg in ((0, 1), (1, -1)):
                    p, q = ref(wrap(p1 - s * sg, n1), p2), ref(wrap(p1 - (s + 1) * sg, n1), p2)
                    if s == n1 // 2 - 1:
                        rows = self.buf.shape[3]
                        cut = pl.ds(0, self.split) if d == 0 else pl.ds(self.split, rows - self.split)
                        p, q = p.at[cut], q.at[cut]
                    step.append((d, p, q, go(first, sg)))
                steps.append(step)
        whole = pl.ds(0, n1)
        shared = {len(steps): [ref(whole, p2)]}
        if self.direct[core][1]:
            steps.append([(k - 1, ref(whole, p2), ref(whole, wrap(p2 - k, n2)), go(second, k)) for k in range(1, n2)])
        else:
            for s in range(n2 // 2):
                step = []
                last = s == n2 // 2 - 1
                for d, sg in ((0, 1), (1, -1)):
                    part = pl.ds(d * (n1 // 2), n1 // 2) if last else whole
                    step.append((d, ref(part, wrap(p2 - s * sg, n2)), ref(part, wrap(p2 - (s + 1) * sg, n2)), go(second, sg)))
                steps.append(step)
                far = [wrap(p2 + s + 1, n2)] if last else [wrap(p2 - s - 1, n2), wrap(p2 + s + 1, n2)]
                shared[len(steps)] = [ref(whole, k) for k in far]
        if self.share == "end":
            shared = {len(steps): [self.buf.at[core]]}
        return steps, (shared if self.share else {})

    def remote(self, ref, s, k, to):
        return pltpu.make_async_remote_copy(
            src_ref=ref, dst_ref=ref, send_sem=self.send.at[self.w, s, k], recv_sem=self.recv.at[self.w, s, k],
            device_id=to, device_id_type=MESH)

    def across(self, ref, k, core):
        return pltpu.make_async_remote_copy(
            src_ref=ref, dst_ref=ref, send_sem=self.dsend.at[self.w, k], recv_sem=self.drecv.at[self.w, k],
            device_id=device(self.y, self.x, 1 - core, self.m), device_id_type=MESH)

    def step(self, s):
        for core in (0, 1):
            steps, shared = self.plan(core)
            if s > len(steps):
                continue

            @pl.when(self.c == core)
            def _():
                if s > 0:
                    for k, _, q, to in steps[s - 1]:
                        self.remote(q, s - 1, k, to).wait_recv()
                if s < len(steps):
                    for k, p, _, to in steps[s]:
                        self.remote(p, s, k, to).start()
                k = 0
                for t, refs in shared.items():
                    for ref in refs:
                        if t == s:
                            self.across(ref, k, core).start()
                        k += 1

    def finish(self):
        for core in (0, 1):
            _, shared = self.plan(1 - core)

            @pl.when(self.c == core)
            def _():
                for k, ref in enumerate([r for refs in shared.values() for r in refs]):
                    self.across(ref, k, core).wait_recv()

    def drain(self):
        for core in (0, 1):
            steps, shared = self.plan(core)

            @pl.when(self.c == core)
            def _():
                for s, step in enumerate(steps):
                    for k, p, _, to in step:
                        self.remote(p, s, k, to).wait_send()
                for k, ref in enumerate([r for refs in shared.values() for r in refs]):
                    self.across(ref, k, core).wait_send()


def z_copies(src, dst, send, recv, first):
    e, m, _, _, _ = place()
    out = []
    for j in range(1, NZ):
        to, back = wrap(m + j, NZ), wrap(m - j, NZ)
        mk = lambda s, d: pltpu.make_async_remote_copy(
            src_ref=s, dst_ref=d, send_sem=send.at[first + j - 1], recv_sem=recv.at[first + j - 1],
            device_id=(e, to), device_id_type=MESH)
        out.append((mk(src(to), dst.at[m]), mk(src(to), dst.at[back])))
    return out


def normed_rows(values, gain, epsilon):
    center = values - jnp.mean(values, axis=-1, keepdims=True)
    spread = jnp.mean(center * center, axis=-1, keepdims=True)
    return center * lax.rsqrt(spread + epsilon) * gain


def whole(feats_h, dw_h, lng, we_h, wc_h, ls, owner_row, tissue, slide_h, sg, wq_h, wk_h, wv_h, wo_h, level, rate, length,
          emb, out,
          feats, dw, we, wc, slide, wq, wk, wv, wo,
          wxs, wxr, wb, wcb, nb, conv, mf, dxs, dxr, zs, zr, exs, exr, ws, wor,
          kvb, metab, fb, keyf, s0, s1, fresh_ref, ab, attn,
          lsem, send, recv, dsend, drecv, msend, mrecv):
    e, m, c, x, y = place()
    other = device(y, x, 1 - c, m)
    targets = [other]
    for sg_ in range(1, NX):
        targets.append(device(y, wrap(x + sg_, NX), c, m))
    for sg_ in range(1, NY):
        targets.append(device(wrap(y + sg_, NY), x, c, m))
    for j in range(1, NZ):
        targets.append((e, wrap(m + j, NZ)))
    barrier = pltpu.get_barrier_semaphore()
    for to in targets:
        pl.semaphore_signal(barrier, inc=1, device_id=to, device_id_type=MESH)

    loads = {}
    for i, (name, src, dst) in enumerate((("we", we_h, we), ("wc", wc_h, wc), ("slide", slide_h, slide), ("wk", wk_h, wk), ("wv", wv_h, wv),
                                          ("feats", feats_h, feats), ("dw", dw_h, dw), ("wo", wo_h, wo), ("wq", wq_h, wq))):
        loads[name] = pltpu.make_async_copy(src, dst, lsem.at[i])
        loads[name].start()
    sems = (send, recv, dsend, drecv)

    def across(src, dst, k):
        return pltpu.make_async_remote_copy(
            src_ref=src, dst_ref=dst, send_sem=msend.at[k], recv_sem=mrecv.at[k], device_id=other, device_id_type=MESH)

    nt = lambda a, b: lax.dot_general(a, b, (((1,), (1,)), ((), ())), preferred_element_type=F32)

    loads["we"].wait()
    loads["wc"].wait()
    for core in (0, 1):

        @pl.when(c == core)
        def _():
            lanes = pl.ds(384 * (1 - core), 384)
            wxs[0] = we[:, lanes].astype(F32)
            wxs[1] = wc[:, lanes].astype(F32)

    loads["slide"].wait()
    loads["wk"].wait()
    loads["wv"].wait()
    gain = sg[...].reshape(1, D)
    snorm = normed_rows(slide[...].astype(F32), gain, 1e-05).astype(BF16)
    for i, ref in enumerate((wk, wv)):
        kvb[c, y, x, pl.ds(96 * i, 96), :] = nt(ref[...], snorm).astype(BF16)

    row = lax.broadcasted_iota(jnp.int32, (16, 128), 0)
    lane = lax.broadcasted_iota(jnp.int32, (16, 128), 1)
    info = jnp.where(row == 0, tissue[:, pl.ds(0, 128)].astype(F32), 0.0)
    info = jnp.where(row == 1, tissue[:, pl.ds(128, 128)].astype(F32), info)
    own = owner_row[...].astype(F32)
    for i in range(4):
        info = jnp.where((row - 2) * 128 + lane == 4 * e + i, own[:, i:i + 1], info)
    metab[c, y, x] = info.astype(BF16)

    pl.semaphore_wait(barrier, len(targets))
    cross_w = across(wxs, wxr, 0)
    cross_w.start()
    mixed = ("xy", "yx")
    g_w = Gather(0, wb, sems, mixed, ((True, False), (True, False)))
    g_wc = Gather(1, wcb, sems, mixed, ((True, False), (True, False)))
    g_kv = Gather(2, kvb, sems, mixed, ((True, False), (False, False)), 96, "step")
    g_meta = Gather(3, metab, sems, mixed, ((True, True), (True, True)), share="end")
    g_f = Gather(4, fb, sems, mixed, ((True, True), (True, True)), share="end")
    g_meta.step(0)
    cross_w.wait()
    for core in (0, 1):

        @pl.when(c == core)
        def _():
            lanes = pl.ds(384 * core, 384)
            for k, (src, dst) in enumerate(((we, wb), (wc, wcb))):
                mine = src[:, lanes].astype(F32)
                pair = [mine, wxr[k]] if core == 0 else [wxr[k], mine]
                dst[0, y, x] = jnp.concatenate(pair, axis=0).astype(BF16)

    g_w.step(0)
    g_wc.step(0)
    g_kv.step(0)

    loads["wo"].wait()
    for j in range(NZ):
        ws[j] = wo[:, 192 * j:192 * j + 192]
    wor[m] = ws[m]
    wo_copies = z_copies(lambda to: ws.at[to], wor, msend, mrecv, 16)
    for copy, _ in wo_copies:
        copy.start()

    loads["feats"].wait()
    loads["dw"].wait()
    sub = lax.broadcasted_iota(jnp.int32, (8, 8, 128), 1)

    def conv_tile(t):
        def chunk(k, carry):
            lanes = pl.ds(pl.multiple_of(k * 128, 128), 128)
            xs = feats[t, :, :, lanes].astype(F32)
            mf[pl.ds(t, 1), lanes] = jnp.sum(jnp.sum(xs, axis=0), axis=0, keepdims=True)
            weight = dw[:, :, lanes].astype(F32)
            total = [jnp.zeros((8, 128), F32)] * 8
            for col in range(7):
                off = col - 3
                if off == 0:
                    moved = xs
                else:
                    moved = pltpu.roll(xs, (-off) % 8, axis=1)
                    moved = jnp.where((sub + off >= 0) & (sub + off < 8), moved, 0.0)
                for r in range(7):
                    tap = weight[r, col:col + 1, :]
                    for h in range(8):
                        if 0 <= h + r - 3 < 8:
                            total[h] = total[h] + moved[h + r - 3] * tap
            for h in range(8):
                conv[pl.ds(8 * h, 8), lanes] = total[h]
            return carry

        lax.fori_loop(0, D // 128, chunk, 0)
        nb[c, pl.ds(64 * t, 64), :] = normed_rows(conv[...], lng[...].reshape(1, D), 1e-06).astype(BF16)

    def cross_n(t):
        ref = nb.at[c, pl.ds(64 * t, 64)]
        return across(ref, ref, 1 + t)

    after = {0: ((g_w, 1), (g_wc, 1), (g_meta, 1)), 1: ((g_w, 2), (g_wc, 2), (g_kv, 1)), 2: ((g_w, 3), (g_wc, 3), (g_meta, 2)),
             3: ((g_w, 4), (g_wc, 4), (g_kv, 2), (g_w, 5), (g_wc, 5))}
    for t in range(4):
        conv_tile(t)
        cross_n(t).start()
        for g, s in after[t]:
            g.step(s)
    g_kv.step(3)
    for t in range(4):
        cross_n(t).wait_send()
        ref = nb.at[1 - c, pl.ds(64 * t, 64)]
        across(ref, ref, 1 + t).wait_recv()

    sums = []
    wfull = wb[0].reshape(D, 384)
    for k in range(4):
        pre = jnp.dot(nb[k // 2, pl.ds(128 * (k % 2), 128), :], wfull, preferred_element_type=F32)
        act = (0.5 * pre * (1.0 + lax.erf(pre * (0.5 ** 0.5)))).astype(BF16).astype(F32)
        for i in range(2):
            sums.append(jnp.sum(act[64 * i:64 * i + 64], axis=0, keepdims=True))
    hsum = jnp.concatenate(sums, axis=0)
    high = hsum.astype(BF16)
    low = (hsum - high.astype(F32)).astype(BF16)
    part = nt(high, wcb[0].reshape(D, 384)) + nt(low, wcb[0].reshape(D, 384))
    part = part * (ls[...].reshape(1, D) * (1.0 / 64.0))
    mine = mf[...] * (1.0 / 512.0)
    for core in (0, 1):

        @pl.when(c == core)
        def _():
            blank = jnp.zeros((4, D), F32)
            both = part + jnp.concatenate([mine, blank] if core == 0 else [blank, mine], axis=0)
            zs[...] = both[:, 768 * core:768 * core + 768]
            dxs[...] = both[:, 768 * (1 - core):768 * (1 - core) + 768]

    cross_p = across(dxs, dxr, 5)
    cross_p.start()
    g_kv.step(4)
    cross_p.wait()
    zs[...] = zs[...] + dxr[...]
    zr[m] = zs[...]
    zc = z_copies(lambda to: zs, zr, msend, mrecv, 8)
    for copy, _ in zc:
        copy.start()

    g_meta.finish()
    info = [metab[k].reshape(32, 16, 128).astype(F32) for k in range(2)]
    owner = jnp.concatenate([sum(jnp.sum(i[:, 2 + k, :], axis=0, keepdims=True) for i in info) for k in range(2)], axis=1)
    strip_of = 2 * lax.broadcasted_iota(jnp.int32, (32, 256), 0)
    picks, spots = [], 0.0
    for k in range(2):
        rows = jnp.concatenate([info[k][:, 0, :], info[k][:, 1, :]], axis=1)
        pick = ((strip_of + k).astype(F32) == owner).astype(F32)
        picks.append(pick.astype(BF16))
        spots = spots + jnp.sum(pick * rows, axis=0, keepdims=True)
    row_id = lax.broadcasted_iota(jnp.int32, (256, 256), 0).astype(F32)
    at_row = row_id == spots
    at_row_bf = at_row.astype(F32).astype(BF16)
    gone = [nt(p, at_row_bf) for p in picks]

    f = lax.broadcasted_iota(jnp.int32, (32, 256), 0)
    amount = jnp.where(f < 8, 10 + f % 4, jnp.where(f < 14, (f - 8) % 3, (f - 14) % 3))
    flipped = ((f >= 4) & (f < 8)) | ((f >= 11) & (f < 14)) | ((f >= 17) & (f < 20))
    rates = [rate[h].astype(F32) for h in range(2)]
    limit = length[0].astype(F32)

    def bits(pos):
        pos_f = pos.astype(F32)
        res = [(pos_f - r * jnp.floor((pos_f + 0.5) / r)).astype(jnp.int32) for r in rates]
        src = jnp.where(f < 8, pos, jnp.where(f < 14, res[0], res[1]))
        bit = (jnp.right_shift(src, amount) & 1).astype(F32)
        return jnp.where(f < 20, jnp.where(flipped, 1.0 - bit, bit), 0.0)

    def features(pos, dead):
        dead = jnp.where(pos.astype(F32) >= limit, 1.0, dead)
        return jnp.where(f == 20, dead, bits(pos)).astype(BF16)

    line = lax.broadcasted_iota(jnp.int32, (1, 256), 1)
    for k in range(64):
        core, chip = k // 32, k % 32
        keyf[core, chip // NX, chip % NX] = features(line + (2 * chip + core) * 256, gone[core][chip:chip + 1, :])

    qpos = line + e * 256
    qbits = 1.0 - bits(qpos)
    bias = []
    for h in range(2):
        live = (f < 8) & (f % 4 >= 4 - level[h])
        live = live | ((f >= 8 + 6 * h) & (f < 14 + 6 * h)) | (f == 20)
        bias.append(jnp.where(live, qbits * NEG, 0.0).astype(BF16))

    g_kv.step(5)
    for copy, back in zc:
        copy.wait_send()
        back.wait_recv()
    fresh = jnp.sum(zr[...], axis=0)
    exs[...] = fresh
    cross_e = across(exs, exr, 6)
    cross_e.start()
    fb[c, y, x] = jnp.concatenate([fresh[:, :384], fresh[:, 384:]], axis=0).astype(BF16)
    g_f.step(0)
    cross_e.wait()
    for core in (0, 1):

        @pl.when(c == core)
        def _():
            rows = pl.ds(4 * core, 4)
            emb[:, pl.ds(768 * core, 768)] = exs[rows, :].astype(BF16)
            emb[:, pl.ds(768 * (1 - core), 768)] = exr[rows, :].astype(BF16)

    loads["wq"].wait()
    g_f.step(1)
    g_kv.step(6)
    g_f.step(2)
    g_f.finish()

    for k in range(2):
        for h in range(2):
            block = fb[k].reshape(32, 16, 384).astype(F32)[:, 8 * h:8 * h + 8, :]
            fresh_ref[:, pl.ds(768 * k + 384 * h, 384)] = block.reshape(256, 384).astype(BF16)
    rows = fresh_ref[...]
    hits = (at_row & (owner == e.astype(F32))).astype(F32)
    covered = jnp.sum(hits, axis=1, keepdims=True) > 0.5
    placed = jnp.dot(hits.astype(BF16), rows, preferred_element_type=F32)
    strip = jnp.where(covered, placed, slide[...].astype(F32))
    for j in range(NZ):

        @pl.when(m == j)
        def _():
            out[...] = strip[:, 192 * j:192 * j + 192].astype(BF16)

    c2 = HD ** -0.5 * math.log2(math.e)
    query = (nt(wq[...], normed_rows(strip, gain, 1e-05).astype(BF16)) * c2).astype(BF16)
    fnorm = normed_rows(rows.astype(F32), gain, 1e-05).astype(BF16)
    fkey = nt(wk[...], fnorm).astype(BF16)
    fval = nt(wv[...], fnorm).astype(BF16)
    ffeat = features((owner * 256.0 + spots).astype(jnp.int32), jnp.zeros((1, 256), F32))
    blank = jnp.zeros((HD, 256), BF16)
    qaug = jnp.concatenate([jnp.concatenate([query[:HD], blank, bias[0]], axis=0),
                            jnp.concatenate([blank, query[HD:], bias[1]], axis=0)], axis=1)
    g_kv.finish()

    tn = lambda a, b: lax.dot_general(a, b, (((0,), (0,)), ((), ())), preferred_element_type=F32)

    def softened(s, state, values):
        top = state[0]
        new = jnp.maximum(top, jnp.max(s, axis=0, keepdims=True))
        p = jnp.exp2(s - new).astype(BF16)
        shrink = jnp.exp2(top - new)
        acc = [state[1 + h] * shrink[:, 256 * h:256 * h + 256]
               + jnp.dot(values[h], p[:, 256 * h:256 * h + 256], preferred_element_type=F32) for h in range(2)]
        return (new, *acc)

    def score(g, ref):
        k, r = g // NY, lax.rem(g, NY)
        keys = jnp.concatenate(
            [jnp.concatenate([kvb[k, r, i, pl.ds(0, 96), :] for i in range(NX)], axis=1),
             jnp.concatenate([keyf[k, r, i] for i in range(NX)], axis=1)], axis=0)
        ref[...] = tn(keys, qaug)

    def soft(g, ref, state):
        k, r = g // NY, lax.rem(g, NY)
        values = []
        for h in range(2):
            v = jnp.concatenate([kvb[k, r, i, pl.ds(96 + HD * h, HD), :] for i in range(NX)], axis=1)
            values.append(jnp.concatenate([v, jnp.ones((16, 1024), BF16)], axis=0))
        return softened(ref[...], state, values)

    state = (jnp.full((1, 512), NEG, F32), jnp.zeros((64, 256), F32), jnp.zeros((64, 256), F32))
    state = softened(tn(jnp.concatenate([fkey, ffeat], axis=0), qaug), state,
                     [jnp.concatenate([fval[HD * h:HD * h + HD], jnp.ones((16, 256), BF16)], axis=0) for h in range(2)])
    score(0, s0)

    def two(i, state):
        score(2 * i + 1, s1)
        state = soft(2 * i, s0, state)
        score(jnp.minimum(2 * i + 2, 15), s0)
        return soft(2 * i + 1, s1, state)

    _, *acc = lax.fori_loop(0, 8, two, state)
    for h in range(2):
        total = acc[h][HD:HD + 1]
        head = acc[h][:HD] / jnp.where(total > 0, total, 1.0)
        attn[pl.ds(HD * h, HD), :] = jnp.where(qpos.astype(F32) < limit, head, 0.0).astype(BF16)

    ab[m] = attn[...]
    copies = z_copies(lambda to: attn, ab, msend, mrecv, 24)
    for copy, _ in copies:
        copy.start()
    for copy, back in wo_copies:
        copy.wait_send()
        back.wait_recv()
    for g in (g_w, g_wc, g_kv, g_meta, g_f):
        g.drain()
    for copy, back in copies:
        copy.wait_send()
        back.wait_recv()
    total = tn(ab[...].reshape(768, 256), wor[...].reshape(768, 192))
    out[...] = (out[...].astype(F32) + total).astype(BF16)


VM = pl.BlockSpec(memory_space=pltpu.VMEM)
SM = pl.BlockSpec(memory_space=pltpu.SMEM)
ANY = pl.BlockSpec(memory_space=pl.ANY)


def shape(dims, dtype=BF16):
    return jax.ShapeDtypeStruct(dims, dtype)


def body(tile_feats, dw_weight, ln_gain, w_expand, w_contract, layer_scale, tile_owner, tissue_index, slide_embed,
         slide_gain, w_query, w_key, w_value, w_out, segment_level, dilate_rate, slide_length):
    dma = pltpu.SemaphoreType.DMA
    vm = lambda dims, dtype=BF16: pltpu.VMEM(dims, dtype)
    return pl.pallas_call(
        whole,
        out_shape=[shape((4, D)), shape((256, 192))],
        in_specs=[ANY, ANY, VM, ANY, ANY, VM, VM, VM, ANY, VM, ANY, ANY, ANY, ANY, SM, SM, SM],
        out_specs=[VM] * 2,
        scratch_shapes=[
            vm((4, 8, 8, D)), vm((7, 7, D)), vm((24, 768)), vm((24, 768)), vm((256, D)), vm((96, D)), vm((96, D)), vm((96, D)), vm((96, D)),
            vm((2, 24, 384), F32), vm((2, 24, 384), F32),
            vm((1, 8, 4, 48, 384)), vm((1, 8, 4, 48, 384)),
            vm((2, 256, D)), vm((64, D), F32), vm((4, D), F32),
            vm((8, 768), F32), vm((8, 768), F32), vm((8, 768), F32), vm((8, 8, 768), F32),
            vm((8, 768), F32), vm((8, 768), F32), vm((8, 96, 192)), vm((8, 96, 192)),
            vm((2, 8, 4, 192, 256)), vm((2, 8, 4, 16, 128)), vm((2, 8, 4, 16, 384)), vm((2, 8, 4, 32, 256)),
            vm((1024, 512), F32), vm((1024, 512), F32), vm((256, D)), vm((8, 96, 256)), vm((96, 256)),
            dma((9,)), dma((5, 6, 7)), dma((5, 6, 7)), dma((5, 8)), dma((5, 8)), dma((32,)), dma((32,)),
        ],
        name="whole",
        compiler_params=pltpu.CompilerParams(collective_id=0, has_side_effects=True, vmem_limit_bytes=56 * 2**20),
    )(tile_feats, dw_weight, ln_gain, w_expand, w_contract, layer_scale, tile_owner.T, tissue_index, slide_embed, slide_gain,
      w_query.T, w_key.T, w_value.T, w_out, segment_level, dilate_rate, slide_length)


def solution(mesh):
    placed = (
        P("enc", None, None, None),
        P(),
        P(),
        P("enc", "mdl"),
        P("enc", "mdl"),
        P(),
        P("enc", None),
        P("enc", None),
        P("enc", None),
        P(),
        P(None, "mdl"),
        P(None, "mdl"),
        P(None, "mdl"),
        P("mdl", None),
        P("mdl"),
        P("mdl"),
        P(),
    )
    return jax.shard_map(
        body,
        mesh=mesh,
        in_specs=placed,
        out_specs=(P("enc", None), P("enc", "mdl")),
        check_vma=False,
    )
```

time: 150 us -> 113 us (0.75)
  Pallas kernels: 131 us -> 109 us
  local copies, waits for them, and re-layouts: 16.5 us -> 2.26 us
    pallas_call x3 -> x1, Pallas kernels: 131 us -> 109 us  [body(): pl.pallas_call(whole, out_shape=[shape((4, D)), shape((256, 192))], in_sp...]
    unnamed x26 -> x3, local copies, waits for them, and re-layouts: 14.4 us -> 0.6 us
    reshape x3 -> x0, local copies, waits for them, and re-layouts: 2.1 us -> none  [the longest x1 0.7 us: body(): slide_gain.reshape(1, D)]
    pallas_call x0 -> x1, local copies, waits for them, and re-layouts: none -> 1.65 us  [body(): pl.pallas_call(whole, out_shape=[shape((4, D)), shape((256, 192))], in_sp...]
where the time goes in v2:
time: 113 us; the launch traced here: 112 us
  Pallas kernels  109 us (96%)
  local copies, waits for them, and re-layouts  2.26 us (2%)
  between operations  1.3 us (1%)
    pallas_call x1, Pallas kernels, body(): pl.pallas_call(whole, out_shape=[shape((4, D)), shape((256, 192))], in_sp...  109 us

profile of v2, /device:TPU:1, one launch (start us, length us, event | category | flops | bytes accessed | tf_op | source)
XLA Modules:
  0.0 112.3 jit_solution(8950062684640228426)
XLA Ops:
  1.3 108.8 %whole.1 = (bf16[4,1536]{1,0:T(4,128)(2,1)}, bf16[256,192]{1,0:T(8,128)(2,1)}) custom-call(bf16[4,8,8,1536]{3,2,1,0:T(8,128)(2,1)} %feats_h.1, bf16[7,7,1536]{2,1,0:T(8,128)(2,1)} %dw_h.1, f32[1536]{0:T(1024)} %lng.1, bf16[24,768]{1,0:T(8,128)(2,1)} %we_h.1, bf16[24,768]{1,0:T(8,128)(2,1)} %wc_h.1, f32[1536]{0:T(1024)} %ls.1, s32[1,4]{1,0:T(1,128)} %bitcast.7, ...), custom_call_target="tpu_custom_call" | custom-call | tf_op jit(solution)/shard_map/whole/pallas_call | solution.py:503
  110.1 0.0 copy-start
  110.1 1.7 %copy.19 = bf16[256,192]{0,1:T(8,128)(2,1)} copy(bf16[256,192]{1,0:T(8,128)(2,1)} %get-tuple-element.3) | data formatting | bytes 196608 | tf_op jit(solution)/shard_map/whole/pallas_call | solution.py:503
  111.7 0.0 copy-done
  111.7 0.6 copy.22
Async XLA Ops:
  110.1 1.7 %copy-start = (bf16[4,1536]{1,0:T(4,128)(2,1)S(1)}, bf16[4,1536]{1,0:T(4,128)(2,1)}, u32[]{:S(2)}) copy-start(bf16[4,1536]{1,0:T(4,128)(2,1)} %get-tuple-element.6) | copy-start | bytes 36868

commit v3 on v2

--- a/solution.py
+++ b/solution.py
@@ -121,14 +121,17 @@
                             self.across(ref, k, core).start()
                         k += 1
 
+    def wait_shared(self, source):
+        _, shared = self.plan(source)
+        for k, ref in enumerate([r for refs in shared.values() for r in refs]):
+            self.across(ref, k, 1 - source).wait_recv()
+
     def finish(self):
         for core in (0, 1):
-            _, shared = self.plan(1 - core)
 
             @pl.when(self.c == core)
             def _():
-                for k, ref in enumerate([r for refs in shared.values() for r in refs]):
-                    self.across(ref, k, core).wait_recv()
+                self.wait_shared(1 - core)
 
     def drain(self):
         for core in (0, 1):
@@ -164,8 +167,8 @@
 def whole(feats_h, dw_h, lng, we_h, wc_h, ls, owner_row, tissue, slide_h, sg, wq_h, wk_h, wv_h, wo_h, level, rate, length,
           emb, out,
           feats, dw, we, wc, slide, wq, wk, wv, wo,
-          wxs, wxr, wb, wcb, nb, conv, mf, dxs, dxr, zs, zr, exs, exr, ws, wor,
-          kvb, metab, fb, keyf, s0, s1, fresh_ref, ab, attn,
+          wxs, wxr, wb0, wb1, wc0, wc1, nb, conv, mf, dxs, dxr, zs, zb, zr, exs, exr, ws, wor,
+          kvb, metab, fb, keyf, stored_query, s0, s1, four, pick_rows, ab, attn,
           lsem, send, recv, dsend, drecv, msend, mrecv):
     e, m, c, x, y = place()
     other = device(y, x, 1 - c, m)
@@ -206,10 +209,13 @@
     loads["slide"].wait()
     loads["wk"].wait()
     loads["wv"].wait()
+    loads["wq"].wait()
     gain = sg[...].reshape(1, D)
     snorm = normed_rows(slide[...].astype(F32), gain, 1e-05).astype(BF16)
     for i, ref in enumerate((wk, wv)):
         kvb[c, y, x, pl.ds(96 * i, 96), :] = nt(ref[...], snorm).astype(BF16)
+    c2 = HD ** -0.5 * math.log2(math.e)
+    stored_query[...] = (nt(wq[...], snorm) * c2).astype(BF16)
 
     row = lax.broadcasted_iota(jnp.int32, (16, 128), 0)
     lane = lax.broadcasted_iota(jnp.int32, (16, 128), 1)
@@ -224,11 +230,10 @@
     cross_w = across(wxs, wxr, 0)
     cross_w.start()
     mixed = ("xy", "yx")
-    g_w = Gather(0, wb, sems, mixed, ((True, False), (True, False)))
-    g_wc = Gather(1, wcb, sems, mixed, ((True, False), (True, False)))
-    g_kv = Gather(2, kvb, sems, mixed, ((True, False), (False, False)), 96, "step")
-    g_meta = Gather(3, metab, sems, mixed, ((True, True), (True, True)), share="end")
-    g_f = Gather(4, fb, sems, mixed, ((True, True), (True, True)), share="end")
+    g_w = [Gather(i, ref, sems, mixed, ((True, False), (False, False)), 16) for i, ref in enumerate((wb0, wb1, wc0, wc1))]
+    g_kv = Gather(4, kvb, sems, mixed, ((True, False), (False, False)), 96, "step")
+    g_meta = Gather(5, metab, sems, mixed, ((True, True), (True, True)), share="end")
+    g_f = Gather(6, fb, sems, mixed, ((True, True), (True, True)), share="end")
     g_meta.step(0)
     cross_w.wait()
     for core in (0, 1):
@@ -236,13 +241,15 @@
         @pl.when(c == core)
         def _():
             lanes = pl.ds(384 * core, 384)
-            for k, (src, dst) in enumerate(((we, wb), (wc, wcb))):
+            for k, (src, dst) in enumerate(((we, (wb0, wb1)), (wc, (wc0, wc1)))):
                 mine = src[:, lanes].astype(F32)
                 pair = [mine, wxr[k]] if core == 0 else [wxr[k], mine]
-                dst[0, y, x] = jnp.concatenate(pair, axis=0).astype(BF16)
-
-    g_w.step(0)
-    g_wc.step(0)
+                both = jnp.concatenate(pair, axis=0).astype(BF16)
+                dst[0][0, y, x] = both[:, :128]
+                dst[1][0, y, x] = both[:, 128:]
+
+    for g in g_w:
+        g.step(0)
     g_kv.step(0)
 
     loads["wo"].wait()
@@ -287,51 +294,53 @@
         ref = nb.at[c, pl.ds(64 * t, 64)]
         return across(ref, ref, 1 + t)
 
-    after = {0: ((g_w, 1), (g_wc, 1), (g_meta, 1)), 1: ((g_w, 2), (g_wc, 2), (g_kv, 1)), 2: ((g_w, 3), (g_wc, 3), (g_meta, 2)),
-             3: ((g_w, 4), (g_wc, 4), (g_kv, 2), (g_w, 5), (g_wc, 5))}
+    after = {0: [(g, 1) for g in g_w] + [(g_meta, 1)], 1: [(g, 2) for g in g_w] + [(g_kv, 1)], 2: [(g, 3) for g in g_w] + [(g_meta, 2)],
+             3: [(g, 4) for g in g_w] + [(g_kv, 2)] + [(g, t) for t in (5, 6) for g in g_w]}
     for t in range(4):
         conv_tile(t)
         cross_n(t).start()
         for g, s in after[t]:
             g.step(s)
-    g_kv.step(3)
     for t in range(4):
         cross_n(t).wait_send()
         ref = nb.at[1 - c, pl.ds(64 * t, 64)]
         across(ref, ref, 1 + t).wait_recv()
 
     sums = []
-    wfull = wb[0].reshape(D, 384)
     for k in range(4):
-        pre = jnp.dot(nb[k // 2, pl.ds(128 * (k % 2), 128), :], wfull, preferred_element_type=F32)
+        rows = nb[k // 2, pl.ds(128 * (k % 2), 128), :]
+        pre = jnp.concatenate([jnp.dot(rows, ref[0].reshape(D, -1), preferred_element_type=F32) for ref in (wb0, wb1)], axis=1)
         act = (0.5 * pre * (1.0 + lax.erf(pre * (0.5 ** 0.5)))).astype(BF16).astype(F32)
         for i in range(2):
             sums.append(jnp.sum(act[64 * i:64 * i + 64], axis=0, keepdims=True))
     hsum = jnp.concatenate(sums, axis=0)
     high = hsum.astype(BF16)
     low = (hsum - high.astype(F32)).astype(BF16)
-    part = nt(high, wcb[0].reshape(D, 384)) + nt(low, wcb[0].reshape(D, 384))
+    part = 0.0
+    for half in (high, low):
+        part += nt(half[:, :128], wc0[0].reshape(D, 128)) + nt(half[:, 128:], wc1[0].reshape(D, 256))
     part = part * (ls[...].reshape(1, D) * (1.0 / 64.0))
-    mine = mf[...] * (1.0 / 512.0)
+    mine = mf[...] * (1.0 / 64.0)
     for core in (0, 1):
 
         @pl.when(c == core)
         def _():
-            blank = jnp.zeros((4, D), F32)
-            both = part + jnp.concatenate([mine, blank] if core == 0 else [blank, mine], axis=0)
-            zs[...] = both[:, 768 * core:768 * core + 768]
-            dxs[...] = both[:, 768 * (1 - core):768 * (1 - core) + 768]
+            zs[...] = part[:, 768 * core:768 * core + 768]
+            far = slice(768 * (1 - core), 768 * (1 - core) + 768)
+            dxs[...] = jnp.concatenate([part[:, far], mine[:, far], jnp.zeros((4, 768), F32)], axis=0)
 
     cross_p = across(dxs, dxr, 5)
     cross_p.start()
-    g_kv.step(4)
     cross_p.wait()
-    zs[...] = zs[...] + dxr[...]
-    zr[m] = zs[...]
-    zc = z_copies(lambda to: zs, zr, msend, mrecv, 8)
+    both = zs[...] + dxr[pl.ds(0, 8), :]
+    zb[...] = jnp.concatenate([both[:, :384], both[:, 384:]], axis=0).astype(BF16)
+    zr[m] = zb[...]
+    four[...] = jnp.zeros((8, D), F32)
+    zc = z_copies(lambda to: zb, zr, msend, mrecv, 8)
     for copy, _ in zc:
         copy.start()
 
+    g_kv.step(3)
     g_meta.finish()
     info = [metab[k].reshape(32, 16, 128).astype(F32) for k in range(2)]
     owner = jnp.concatenate([sum(jnp.sum(i[:, 2 + k, :], axis=0, keepdims=True) for i in info) for k in range(2)], axis=1)
@@ -347,6 +356,15 @@
     at_row_bf = at_row.astype(F32).astype(BF16)
     gone = [nt(p, at_row_bf) for p in picks]
 
+    hits = (at_row & (owner == e.astype(F32))).astype(F32).astype(BF16)
+    covered = nt(jnp.ones((8, 256), BF16), hits)
+
+    shard = lax.broadcasted_iota(jnp.int32, (1024, 256), 0)
+    tile = lax.broadcasted_iota(jnp.int32, (1024, 256), 1)
+    tile_row = (tile // 4 % 2) * 512 + tile // 8 * 16 + tile % 4
+    for k in range(4):
+        pick_rows[:, pl.ds(256 * k, 256)] = (shard == tile_row + 4 * k).astype(F32).astype(BF16)
+
     f = lax.broadcasted_iota(jnp.int32, (32, 256), 0)
     amount = jnp.where(f < 8, 10 + f % 4, jnp.where(f < 14, (f - 8) % 3, (f - 14) % 3))
     flipped = ((f >= 4) & (f < 8)) | ((f >= 11) & (f < 14)) | ((f >= 17) & (f < 20))
@@ -377,59 +395,58 @@
         live = live | ((f >= 8 + 6 * h) & (f < 14 + 6 * h)) | (f == 20)
         bias.append(jnp.where(live, qbits * NEG, 0.0).astype(BF16))
 
-    g_kv.step(5)
+    g_kv.step(4)
     for copy, back in zc:
         copy.wait_send()
         back.wait_recv()
-    fresh = jnp.sum(zr[...], axis=0)
-    exs[...] = fresh
+    summed = jnp.sum(zr[...].astype(F32), axis=0)
+    for core in (0, 1):
+
+        @pl.when(c == core)
+        def _():
+            pair = [mine[:, 768 * core:768 * core + 768], dxr[pl.ds(8, 4), :]]
+            exs[...] = jnp.concatenate([summed[:8], summed[8:]], axis=1) + jnp.concatenate(pair if core == 0 else pair[::-1], axis=0)
+
     cross_e = across(exs, exr, 6)
     cross_e.start()
-    fb[c, y, x] = jnp.concatenate([fresh[:, :384], fresh[:, 384:]], axis=0).astype(BF16)
-    g_f.step(0)
     cross_e.wait()
     for core in (0, 1):
 
         @pl.when(c == core)
         def _():
-            rows = pl.ds(4 * core, 4)
-            emb[:, pl.ds(768 * core, 768)] = exs[rows, :].astype(BF16)
-            emb[:, pl.ds(768 * (1 - core), 768)] = exr[rows, :].astype(BF16)
-
-    loads["wq"].wait()
+            at = pl.ds(4 * core, 4)
+            pair = [exs[at, :], exr[at, :]]
+            four[pl.ds(0, 4), :] = jnp.concatenate(pair if core == 0 else pair[::-1], axis=1)
+
+    mine4 = four[...].astype(BF16)
+    emb[...] = mine4[:4]
+    norm4 = normed_rows(mine4.astype(F32), gain, 1e-05).astype(BF16)
+    k4, v4, q4 = nt(norm4, wk[...])[:4], nt(norm4, wv[...])[:4], (nt(norm4, wq[...]) * c2)[:4]
+    for j in range(NZ):
+
+        @pl.when(m == j)
+        def _():
+            cols = mine4.astype(F32)[:4, 192 * j:192 * j + 192]
+            block = [jnp.concatenate([k4, cols[:, 128:160]], axis=1), jnp.concatenate([v4, cols[:, 160:192]], axis=1),
+                     jnp.concatenate([q4, jnp.zeros((4, 32), F32)], axis=1), cols[:, :128]]
+            fb[c, y, x] = jnp.concatenate(block, axis=0).astype(BF16)
+
+    g_f.step(0)
+    g_kv.step(5)
     g_f.step(1)
-    g_kv.step(6)
     g_f.step(2)
     g_f.finish()
 
-    for k in range(2):
-        for h in range(2):
-            block = fb[k].reshape(32, 16, 384).astype(F32)[:, 8 * h:8 * h + 8, :]
-            fresh_ref[:, pl.ds(768 * k + 384 * h, 384)] = block.reshape(256, 384).astype(BF16)
-    rows = fresh_ref[...]
-    hits = (at_row & (owner == e.astype(F32))).astype(F32)
-    covered = jnp.sum(hits, axis=1, keepdims=True) > 0.5
-    placed = jnp.dot(hits.astype(BF16), rows, preferred_element_type=F32)
-    strip = jnp.where(covered, placed, slide[...].astype(F32))
-    for j in range(NZ):
-
-        @pl.when(m == j)
-        def _():
-            out[...] = strip[:, 192 * j:192 * j + 192].astype(BF16)
-
-    c2 = HD ** -0.5 * math.log2(math.e)
-    query = (nt(wq[...], normed_rows(strip, gain, 1e-05).astype(BF16)) * c2).astype(BF16)
-    fnorm = normed_rows(rows.astype(F32), gain, 1e-05).astype(BF16)
-    fkey = nt(wk[...], fnorm).astype(BF16)
-    fval = nt(wv[...], fnorm).astype(BF16)
+    tn = lambda a, b: lax.dot_general(a, b, (((0,), (0,)), ((), ())), preferred_element_type=F32)
+    every = tn(fb[...].reshape(1024, 128), pick_rows[...]).astype(BF16)
+    fkey, fval = every[:96, :256], every[:96, 256:512]
+    fresh_cols = jnp.concatenate([every[:, 768:], every[96:, :256], every[96:, 256:512]], axis=0)
+    query = nt(every[:96, 512:768], hits)
+    query = jnp.where(covered[:1] > 0.5, query, stored_query[...].astype(F32)).astype(BF16)
     ffeat = features((owner * 256.0 + spots).astype(jnp.int32), jnp.zeros((1, 256), F32))
     blank = jnp.zeros((HD, 256), BF16)
     qaug = jnp.concatenate([jnp.concatenate([query[:HD], blank, bias[0]], axis=0),
                             jnp.concatenate([blank, query[HD:], bias[1]], axis=0)], axis=1)
-    g_kv.finish()
-
-    tn = lambda a, b: lax.dot_general(a, b, (((0,), (0,)), ((), ())), preferred_element_type=F32)
-
     def softened(s, state, values):
         top = state[0]
         new = jnp.maximum(top, jnp.max(s, axis=0, keepdims=True))
@@ -439,33 +456,57 @@
                + jnp.dot(values[h], p[:, 256 * h:256 * h + 256], preferred_element_type=F32) for h in range(2)]
         return (new, *acc)
 
-    def score(g, ref):
-        k, r = g // NY, lax.rem(g, NY)
+    def near(k):
+        return (k + 1) // 2 * (1 - 2 * lax.rem(k, 2))
+
+    def by_row(g, i):
+        return 0, wrap(y + near(g), NY), i
+
+    def by_column(g, i):
+        return 1, 4 * lax.rem(g, 2) + i, wrap(x + near(g // 2), NX)
+
+    def score(at, g, ref):
+        places = [at(g, i) for i in range(4)]
         keys = jnp.concatenate(
-            [jnp.concatenate([kvb[k, r, i, pl.ds(0, 96), :] for i in range(NX)], axis=1),
-             jnp.concatenate([keyf[k, r, i] for i in range(NX)], axis=1)], axis=0)
+            [jnp.concatenate([kvb[k, r, q, pl.ds(0, 96), :] for k, r, q in places], axis=1),
+             jnp.concatenate([keyf[k, r, q] for k, r, q in places], axis=1)], axis=0)
         ref[...] = tn(keys, qaug)
 
-    def soft(g, ref, state):
-        k, r = g // NY, lax.rem(g, NY)
+    def soft(at, g, ref, state):
+        places = [at(g, i) for i in range(4)]
         values = []
         for h in range(2):
-            v = jnp.concatenate([kvb[k, r, i, pl.ds(96 + HD * h, HD), :] for i in range(NX)], axis=1)
+            v = jnp.concatenate([kvb[k, r, q, pl.ds(96 + HD * h, HD), :] for k, r, q in places], axis=1)
             values.append(jnp.concatenate([v, jnp.ones((16, 1024), BF16)], axis=0))
         return softened(ref[...], state, values)
+
+    def eight(at, state):
+        score(at, 0, s0)
+
+        def two(i, state):
+            score(at, 2 * i + 1, s1)
+            state = soft(at, 2 * i, s0, state)
+            score(at, jnp.minimum(2 * i + 2, 7), s0)
+            return soft(at, 2 * i + 1, s1, state)
+
+        return lax.fori_loop(0, 4, two, state)
 
     state = (jnp.full((1, 512), NEG, F32), jnp.zeros((64, 256), F32), jnp.zeros((64, 256), F32))
     state = softened(tn(jnp.concatenate([fkey, ffeat], axis=0), qaug), state,
                      [jnp.concatenate([fval[HD * h:HD * h + HD], jnp.ones((16, 256), BF16)], axis=0) for h in range(2)])
-    score(0, s0)
-
-    def two(i, state):
-        score(2 * i + 1, s1)
-        state = soft(2 * i, s0, state)
-        score(jnp.minimum(2 * i + 2, 15), s0)
-        return soft(2 * i + 1, s1, state)
-
-    _, *acc = lax.fori_loop(0, 8, two, state)
+
+    @pl.when(c == 1)
+    def _():
+        g_kv.wait_shared(0)
+
+    state = eight(by_row, state)
+    g_kv.step(6)
+
+    @pl.when(c == 0)
+    def _():
+        g_kv.wait_shared(1)
+
+    _, *acc = eight(by_column, state)
     for h in range(2):
         total = acc[h][HD:HD + 1]
         head = acc[h][:HD] / jnp.where(total > 0, total, 1.0)
@@ -475,15 +516,22 @@
     copies = z_copies(lambda to: attn, ab, msend, mrecv, 24)
     for copy, _ in copies:
         copy.start()
+    placed = nt(fresh_cols, hits)
+    for j in range(NZ):
+
+        @pl.when(m == j)
+        def _():
+            out[...] = jnp.where(covered[:1] > 0.5, placed, slide[:, 192 * j:192 * j + 192].astype(F32).T).astype(BF16)
+
     for copy, back in wo_copies:
         copy.wait_send()
         back.wait_recv()
-    for g in (g_w, g_wc, g_kv, g_meta, g_f):
+    for g in (*g_w, g_kv, g_meta, g_f):
         g.drain()
     for copy, back in copies:
         copy.wait_send()
         back.wait_recv()
-    total = tn(ab[...].reshape(768, 256), wor[...].reshape(768, 192))
+    total = tn(wor[...].reshape(768, 192), ab[...].reshape(768, 256))
     out[...] = (out[...].astype(F32) + total).astype(BF16)
 
 
@@ -500,26 +548,27 @@
          slide_gain, w_query, w_key, w_value, w_out, segment_level, dilate_rate, slide_length):
     dma = pltpu.SemaphoreType.DMA
     vm = lambda dims, dtype=BF16: pltpu.VMEM(dims, dtype)
-    return pl.pallas_call(
+    emb, out = pl.pallas_call(
         whole,
-        out_shape=[shape((4, D)), shape((256, 192))],
+        out_shape=[shape((4, D)), shape((192, 256))],
         in_specs=[ANY, ANY, VM, ANY, ANY, VM, VM, VM, ANY, VM, ANY, ANY, ANY, ANY, SM, SM, SM],
         out_specs=[VM] * 2,
         scratch_shapes=[
             vm((4, 8, 8, D)), vm((7, 7, D)), vm((24, 768)), vm((24, 768)), vm((256, D)), vm((96, D)), vm((96, D)), vm((96, D)), vm((96, D)),
             vm((2, 24, 384), F32), vm((2, 24, 384), F32),
-            vm((1, 8, 4, 48, 384)), vm((1, 8, 4, 48, 384)),
+            vm((1, 8, 4, 48, 128)), vm((1, 8, 4, 48, 256)), vm((1, 8, 4, 48, 128)), vm((1, 8, 4, 48, 256)),
             vm((2, 256, D)), vm((64, D), F32), vm((4, D), F32),
-            vm((8, 768), F32), vm((8, 768), F32), vm((8, 768), F32), vm((8, 8, 768), F32),
+            vm((16, 768), F32), vm((16, 768), F32), vm((8, 768), F32), vm((16, 384)), vm((8, 16, 384)),
             vm((8, 768), F32), vm((8, 768), F32), vm((8, 96, 192)), vm((8, 96, 192)),
-            vm((2, 8, 4, 192, 256)), vm((2, 8, 4, 16, 128)), vm((2, 8, 4, 16, 384)), vm((2, 8, 4, 32, 256)),
-            vm((1024, 512), F32), vm((1024, 512), F32), vm((256, D)), vm((8, 96, 256)), vm((96, 256)),
-            dma((9,)), dma((5, 6, 7)), dma((5, 6, 7)), dma((5, 8)), dma((5, 8)), dma((32,)), dma((32,)),
+            vm((2, 8, 4, 192, 256)), vm((2, 8, 4, 16, 128)), vm((2, 8, 4, 16, 128)), vm((2, 8, 4, 32, 256)), vm((96, 256)),
+            vm((1024, 512), F32), vm((1024, 512), F32), vm((8, D), F32), vm((1024, 1024)), vm((8, 96, 256)), vm((96, 256)),
+            dma((9,)), dma((7, 6, 7)), dma((7, 6, 7)), dma((7, 8)), dma((7, 8)), dma((32,)), dma((32,)),
         ],
         name="whole",
         compiler_params=pltpu.CompilerParams(collective_id=0, has_side_effects=True, vmem_limit_bytes=56 * 2**20),
     )(tile_feats, dw_weight, ln_gain, w_expand, w_contract, layer_scale, tile_owner.T, tissue_index, slide_embed, slide_gain,
       w_query.T, w_key.T, w_value.T, w_out, segment_level, dilate_rate, slide_length)
+    return emb, out.T
 
 
 def solution(mesh):

time: 113 us -> 103 us (0.912)
  Pallas kernels: 109 us -> 98.1 us
    pallas_call x1, Pallas kernels: 109 us -> 98.1 us  [body(): pl.pallas_call(whole, out_shape=[shape((4, D)), shape((192, 256))], in_sp...]
    unnamed x3 -> x2, local copies, waits for them, and re-layouts: 0.6 us -> 2.85 us
    pallas_call x1 -> x0, local copies, waits for them, and re-layouts: 1.65 us -> none  [body(): pl.pallas_call(whole, out_shape=[shape((4, D)), shape((256, 192))], in_sp...]
where the time goes in v3:
time: 103 us; the launch traced here: 102 us
  Pallas kernels  98.1 us (95%)
  local copies, waits for them, and re-layouts  2.85 us (3%)
  between operations  1.29 us (1%)
    pallas_call x1, Pallas kernels, body(): pl.pallas_call(whole, out_shape=[shape((4, D)), shape((192, 256))], in_sp...  98.1 us
    unnamed x2, local copies, waits for them, and re-layouts  2.85 us

profile of v3, /device:TPU:1, one launch (start us, length us, event | category | flops | bytes accessed | tf_op | source)
XLA Modules:
  0.0 102.3 jit_solution(3993183108265296097)
XLA Ops:
  1.3 98.1 %whole.1 = (bf16[4,1536]{1,0:T(4,128)(2,1)}, bf16[192,256]{1,0:T(8,128)(2,1)}) custom-call(bf16[4,8,8,1536]{3,2,1,0:T(8,128)(2,1)} %feats_h.1, bf16[7,7,1536]{2,1,0:T(8,128)(2,1)} %dw_h.1, f32[1536]{0:T(1024)} %lng.1, bf16[24,768]{1,0:T(8,128)(2,1)} %we_h.1, bf16[24,768]{1,0:T(8,128)(2,1)} %wc_h.1, f32[1536]{0:T(1024)} %ls.1, s32[1,4]{1,0:T(1,128)} %bitcast.9, ...), custom_call_target="tpu_custom_call" | custom-call | tf_op jit(solution)/shard_map/whole/pallas_call | solution.py:551
  99.4 1.3 %copy.22 = bf16[4,1536]{1,0:T(4,128)(2,1)} copy(bf16[4,1536]{1,0:T(4,128)(2,1)} %get-tuple-element.8) | data formatting | bytes 24576
  100.7 1.5 %copy.23 = bf16[256,192]{0,1:T(8,128)(2,1)} copy(bf16[256,192]{0,1:T(8,128)(2,1)} %bitcast.8) | data formatting | bytes 196608

commit v4 on v3

--- a/solution.py
+++ b/solution.py
@@ -32,13 +32,16 @@
 
 
 class Gather:
-    def __init__(self, wave, buf, sems, orders, direct, split=None, share=""):
+    def __init__(self, wave, buf, sems, orders, direct, split=None, share="", rows=None):
         self.w, self.buf, self.orders, self.direct, self.split, self.share = wave, buf, orders, direct, split, share
+        self.rows = rows
         self.send, self.recv, self.dsend, self.drecv = sems
         self.e, self.m, self.c, self.x, self.y = place()
 
     def at(self, core, y, x):
-        return self.buf.at[core if self.share else 0, y, x]
+        if self.rows is None:
+            return self.buf.at[core if self.share else 0, y, x]
+        return self.buf.at[core if self.share else 0, y, x, pl.ds(*self.rows)]
 
     def own(self):
         return (self.c if self.share else 0, self.y, self.x)
@@ -67,7 +70,7 @@
                 for d, sg in ((0, 1), (1, -1)):
                     p, q = ref(wrap(p1 - s * sg, n1), p2), ref(wrap(p1 - (s + 1) * sg, n1), p2)
                     if s == n1 // 2 - 1:
-                        rows = self.buf.shape[3]
+                        rows = self.rows[1] if self.rows else self.buf.shape[3]
                         cut = pl.ds(0, self.split) if d == 0 else pl.ds(self.split, rows - self.split)
                         p, q = p.at[cut], q.at[cut]
                     step.append((d, p, q, go(first, sg)))
@@ -231,7 +234,7 @@
     cross_w.start()
     mixed = ("xy", "yx")
     g_w = [Gather(i, ref, sems, mixed, ((True, False), (False, False)), 16) for i, ref in enumerate((wb0, wb1, wc0, wc1))]
-    g_kv = Gather(4, kvb, sems, mixed, ((True, False), (False, False)), 96, "step")
+    g_k, g_v = [Gather(4 + 3 * i, kvb, sems, mixed, ((True, False), (False, False)), 48, "step", (96 * i, 96)) for i in range(2)]
     g_meta = Gather(5, metab, sems, mixed, ((True, True), (True, True)), share="end")
     g_f = Gather(6, fb, sems, mixed, ((True, True), (True, True)), share="end")
     g_meta.step(0)
@@ -250,7 +253,8 @@
 
     for g in g_w:
         g.step(0)
-    g_kv.step(0)
+    g_k.step(0)
+    g_v.step(0)
 
     loads["wo"].wait()
     for j in range(NZ):
@@ -294,8 +298,8 @@
         ref = nb.at[c, pl.ds(64 * t, 64)]
         return across(ref, ref, 1 + t)
 
-    after = {0: [(g, 1) for g in g_w] + [(g_meta, 1)], 1: [(g, 2) for g in g_w] + [(g_kv, 1)], 2: [(g, 3) for g in g_w] + [(g_meta, 2)],
-             3: [(g, 4) for g in g_w] + [(g_kv, 2)] + [(g, t) for t in (5, 6) for g in g_w]}
+    after = {0: [(g, 1) for g in g_w] + [(g_meta, 1)], 1: [(g, 2) for g in g_w] + [(g_k, 1), (g_v, 1)], 2: [(g, 3) for g in g_w] + [(g_meta, 2)],
+             3: [(g, 4) for g in g_w] + [(g_k, 2), (g_v, 2)] + [(g, t) for t in (5, 6) for g in g_w]}
     for t in range(4):
         conv_tile(t)
         cross_n(t).start()
@@ -340,7 +344,8 @@
     for copy, _ in zc:
         copy.start()
 
-    g_kv.step(3)
+    g_k.step(3)
+    g_v.step(3)
     g_meta.finish()
     info = [metab[k].reshape(32, 16, 128).astype(F32) for k in range(2)]
     owner = jnp.concatenate([sum(jnp.sum(i[:, 2 + k, :], axis=0, keepdims=True) for i in info) for k in range(2)], axis=1)
@@ -395,7 +400,8 @@
         live = live | ((f >= 8 + 6 * h) & (f < 14 + 6 * h)) | (f == 20)
         bias.append(jnp.where(live, qbits * NEG, 0.0).astype(BF16))
 
-    g_kv.step(4)
+    g_k.step(4)
+    g_v.step(4)
     for copy, back in zc:
         copy.wait_send()
         back.wait_recv()
@@ -432,8 +438,9 @@
             fb[c, y, x] = jnp.concatenate(block, axis=0).astype(BF16)
 
     g_f.step(0)
-    g_kv.step(5)
     g_f.step(1)
+    g_k.step(5)
+    g_v.step(5)
     g_f.step(2)
     g_f.finish()
 
@@ -497,14 +504,17 @@
 
     @pl.when(c == 1)
     def _():
-        g_kv.wait_shared(0)
+        g_k.wait_shared(0)
+        g_v.wait_shared(0)
 
     state = eight(by_row, state)
-    g_kv.step(6)
+    g_k.step(6)
+    g_v.step(6)
 
     @pl.when(c == 0)
     def _():
-        g_kv.wait_shared(1)
+        g_k.wait_shared(1)
+        g_v.wait_shared(1)
 
     _, *acc = eight(by_column, state)
     for h in range(2):
@@ -526,7 +536,7 @@
     for copy, back in wo_copies:
         copy.wait_send()
         back.wait_recv()
-    for g in (*g_w, g_kv, g_meta, g_f):
+    for g in (*g_w, g_k, g_v, g_meta, g_f):
         g.drain()
     for copy, back in copies:
         copy.wait_send()
@@ -562,7 +572,7 @@
             vm((8, 768), F32), vm((8, 768), F32), vm((8, 96, 192)), vm((8, 96, 192)),
             vm((2, 8, 4, 192, 256)), vm((2, 8, 4, 16, 128)), vm((2, 8, 4, 16, 128)), vm((2, 8, 4, 32, 256)), vm((96, 256)),
             vm((1024, 512), F32), vm((1024, 512), F32), vm((8, D), F32), vm((1024, 1024)), vm((8, 96, 256)), vm((96, 256)),
-            dma((9,)), dma((7, 6, 7)), dma((7, 6, 7)), dma((7, 8)), dma((7, 8)), dma((32,)), dma((32,)),
+            dma((9,)), dma((8, 6, 7)), dma((8, 6, 7)), dma((8, 8)), dma((8, 8)), dma((32,)), dma((32,)),
         ],
         name="whole",
         compiler_params=pltpu.CompilerParams(collective_id=0, has_side_effects=True, vmem_limit_bytes=56 * 2**20),

time: 103 us -> 102 us (level)
  Pallas kernels: 98.1 us -> 96.2 us
    pallas_call x1, Pallas kernels: 98.1 us -> 96.2 us  [body(): pl.pallas_call(whole, out_shape=[shape((4, D)), shape((192, 256))], in_sp...]
where the time goes in v4:
time: 102 us; the launch traced here: 100 us
  Pallas kernels  96.2 us (94%)
  local copies, waits for them, and re-layouts  2.85 us (3%)
  between operations  1.29 us (1%)
    pallas_call x1, Pallas kernels, body(): pl.pallas_call(whole, out_shape=[shape((4, D)), shape((192, 256))], in_sp...  96.2 us
    unnamed x2, local copies, waits for them, and re-layouts  2.85 us

profile of v4, /device:TPU:1, one launch (start us, length us, event | category | flops | bytes accessed | tf_op | source)
XLA Modules:
  0.0 100.3 jit_solution(6700949345415642642)
XLA Ops:
  1.3 96.2 %whole.1 = (bf16[4,1536]{1,0:T(4,128)(2,1)}, bf16[192,256]{1,0:T(8,128)(2,1)}) custom-call(bf16[4,8,8,1536]{3,2,1,0:T(8,128)(2,1)} %feats_h.1, bf16[7,7,1536]{2,1,0:T(8,128)(2,1)} %dw_h.1, f32[1536]{0:T(1024)} %lng.1, bf16[24,768]{1,0:T(8,128)(2,1)} %we_h.1, bf16[24,768]{1,0:T(8,128)(2,1)} %wc_h.1, f32[1536]{0:T(1024)} %ls.1, s32[1,4]{1,0:T(1,128)} %bitcast.9, ...), custom_call_target="tpu_custom_call" | custom-call | tf_op jit(solution)/shard_map/whole/pallas_call | solution.py:561
  97.4 1.3 %copy.22 = bf16[4,1536]{1,0:T(4,128)(2,1)} copy(bf16[4,1536]{1,0:T(4,128)(2,1)} %get-tuple-element.8) | data formatting | bytes 24576
  98.8 1.5 %copy.23 = bf16[256,192]{0,1:T(8,128)(2,1)} copy(bf16[256,192]{0,1:T(8,128)(2,1)} %bitcast.8) | data formatting | bytes 196608
